TPU v7x, 32 devices: a whole 2x2x4 slice. The times are simulated.
32 devices in a mesh: seq: 8 (over z, x), tp: 4 (over y, core).
Axes of the slice: x: 2, y: 2, z: 4, core: 2. Of those that a mesh axis runs over, the one named last changes fastest.
Arguments:
- tokens_in: bfloat16 [8, 4, 2560], P(None, None, 'tp'), may hold values from -32 to 32
- attn_gain: bfloat16 [2560], replicated, may hold values from 0.25 to 1.75
- mlp_gain: bfloat16 [2560], replicated, may hold values from 0.25 to 1.75
- proj_query: bfloat16 [2560, 2560], P(None, 'tp'), may hold values from -0.125 to 0.125
- proj_key: bfloat16 [2560, 640], P(None, 'tp'), may hold values from -0.125 to 0.125
- proj_value: bfloat16 [2560, 640], P(None, 'tp'), may hold values from -0.125 to 0.125
- proj_out: bfloat16 [2560, 2560], P('tp'), may hold values from -0.125 to 0.125
- proj_gate: bfloat16 [2560, 3456], P(None, 'tp'), may hold values from -0.125 to 0.125
- proj_up: bfloat16 [2560, 3456], P(None, 'tp'), may hold values from -0.125 to 0.125
- proj_down: bfloat16 [3456, 2560], P('tp'), may hold values from -0.109375 to 0.109375
- long_keys: bfloat16 [4096, 8, 80], P('seq', 'tp'), may hold values from -340 to 340
- long_values: bfloat16 [4096, 8, 80], P('seq', 'tp'), may hold values from -6 to 6
- short_keys: bfloat16 [512, 8, 240], P('seq', 'tp'), may hold values from -340 to 340
- short_values: bfloat16 [512, 8, 240], P('seq', 'tp'), may hold values from -6 to 6
- long_seen: int32 [1], replicated, may hold values from 4096 to 8191
- short_len: int32 [3], replicated, may hold values from 1 to 504, as said below
Outputs:
- layer_out: bfloat16 [8, 4, 2560], P(None, None, 'tp')
Inputs may be any that keep to these rules, and one draw needn't show every extreme that they name: `short_len`: some short request has exactly 504 cached tokens and some exactly 1.
All inputs are finite; a program needn't handle non-finite values.
Results may differ from a plain program's by a relative error of at most 0.01.
Values may be sent and summed in bfloat16 or wider, within the bound.
A program may use at most 128 MiB of HBM per device.

v0:
```python
import math

import jax
import jax.numpy as jnp
from jax import lax
from jax.sharding import PartitionSpec as P

HEADS = 32
KV_HEADS = 8
HD = 80
WIN = 4096
STEPS = 8
LONG = 1


eps_norm = 1e-05
theta_base = 10000.0
masked_score = -1e30


def rms_scaled(hidden_rows, norm_gain):
    mean_square = jnp.mean(hidden_rows * hidden_rows, axis=-1, keepdims=True)
    return hidden_rows * lax.rsqrt(mean_square + eps_norm) * norm_gain.astype(jnp.float32)


def rotate(vectors, positions):
    half_width = vectors.shape[-1] // 2
    freq_index = jnp.arange(half_width, dtype=jnp.float32)
    frequency = theta_base ** (-2.0 * freq_index / vectors.shape[-1])
    angles = positions.astype(jnp.float32)[..., None] * frequency
    view_shape = angles.shape[:2] + (1,) * (vectors.ndim - 3) + (half_width,)
    cosine_table = jnp.cos(angles).reshape(view_shape)
    sine_table = jnp.sin(angles).reshape(view_shape)
    front_part = vectors[..., :half_width]
    back_part = vectors[..., half_width:]
    return jnp.concatenate(
        [
            front_part * cosine_table - back_part * sine_table,
            back_part * cosine_table + front_part * sine_table,
        ],
        axis=-1,
    )


def partial_softmax(queries, cache_keys, cache_values, valid_mask):
    score_scale = 1.0 / math.sqrt(queries.shape[-1])
    scores = (
        jnp.einsum("trkgd,wkrd->trkgw", queries, cache_keys, preferred_element_type=jnp.float32)
        * score_scale
    )
    live_mask = valid_mask[:, :, None, None, :]
    scores = jnp.where(live_mask, scores, masked_score)
    top_score = jnp.max(scores, axis=-1)
    weights = jnp.where(live_mask, jnp.exp(scores - top_score[..., None]), 0.0)
    weight_sum = jnp.sum(weights, axis=-1)
    weighted = jnp.einsum(
        "trkgw,wkrd->trkgd",
        weights.astype(jnp.bfloat16),
        cache_values,
        preferred_element_type=jnp.float32,
    )
    return (top_score, weight_sum, weighted)


def body(
    tokens_in,
    attn_gain,
    mlp_gain,
    proj_query,
    proj_key,
    proj_value,
    proj_out,
    proj_gate,
    proj_up,
    proj_down,
    long_keys,
    long_values,
    short_keys,
    short_values,
    long_seen,
    short_len,
):
    seq_rank = lax.axis_index("seq")
    tp_rank = lax.axis_index("tp")
    local_width = tokens_in.shape[2]
    model_width = proj_query.shape[0]
    total_reqs = tokens_in.shape[1]
    group_size = HEADS // KV_HEADS
    kv_local = proj_key.shape[1] // HD
    base_pos = jnp.concatenate([long_seen, short_len])
    roll_start = long_seen % WIN
    long_slots = long_keys.shape[0]
    short_slots = short_keys.shape[0]
    long_global = seq_rank * long_slots + jnp.arange(long_slots, dtype=jnp.int32)
    long_age = (long_global[None, :] - roll_start[:, None]) % WIN
    short_global = seq_rank * short_slots + jnp.arange(short_slots, dtype=jnp.int32)
    short_live = short_global[None, :] < short_len[:, None]
    long_key_view = long_keys.reshape(long_slots, kv_local, LONG, HD)
    long_value_view = long_values.reshape(long_slots, kv_local, LONG, HD)
    short_key_view = short_keys.reshape(short_slots, kv_local, total_reqs - LONG, HD)
    short_value_view = short_values.reshape(short_slots, kv_local, total_reqs - LONG, HD)
    collected = []
    prior_keys = []
    prior_values = []
    for step_num in range(0, STEPS, STEPS):
        token_rows = tokens_in[step_num : step_num + STEPS]
        block_steps = token_rows.shape[0]
        full_rows = lax.all_gather(token_rows, "tp", axis=2, tiled=True)
        normed = rms_scaled(full_rows.astype(jnp.float32), attn_gain).astype(jnp.bfloat16)
        flat_rows = normed.reshape(block_steps * total_reqs, model_width)
        steps_here = step_num + jnp.arange(block_steps, dtype=jnp.int32)
        positions = steps_here[:, None] + base_pos[None, :]
        queries = jnp.dot(flat_rows, proj_query, preferred_element_type=jnp.float32)
        queries = rotate(
            queries.reshape(block_steps, total_reqs, kv_local, group_size, HD), positions
        ).astype(jnp.bfloat16)
        key_new = jnp.dot(flat_rows, proj_key, preferred_element_type=jnp.float32)
        key_new = rotate(key_new.reshape(block_steps, total_reqs, kv_local, HD), positions).astype(
            jnp.bfloat16
        )
        value_new = jnp.dot(flat_rows, proj_value, preferred_element_type=jnp.float32)
        value_new = value_new.reshape(block_steps, total_reqs, kv_local, HD).astype(jnp.bfloat16)
        every_key = jnp.concatenate(prior_keys + [key_new], axis=0).transpose(0, 2, 1, 3)
        every_value = jnp.concatenate(prior_values + [value_new], axis=0).transpose(0, 2, 1, 3)
        token_ids = jnp.arange(every_key.shape[0], dtype=jnp.int32)
        fresh_valid = jnp.broadcast_to(
            token_ids[None, None, :] <= steps_here[:, None, None],
            (block_steps, total_reqs, every_key.shape[0]),
        )
        long_valid = long_age[None, :, :] > steps_here[:, None, None]
        short_valid = short_live[None]
        long_part = partial_softmax(queries[:, :LONG], long_key_view, long_value_view, long_valid)
        short_part = partial_softmax(
            queries[:, LONG:], short_key_view, short_value_view, short_valid
        )
        old_top = jnp.concatenate([long_part[0], short_part[0]], axis=1)
        old_sum = jnp.concatenate([long_part[1], short_part[1]], axis=1)
        old_acc = jnp.concatenate([long_part[2], short_part[2]], axis=1)
        global_top = lax.pmax(old_top, "seq")
        rescale = jnp.exp(old_top - global_top)
        old_sum, old_acc = lax.psum((old_sum * rescale, old_acc * rescale[..., None]), "seq")
        old_top = global_top
        new_top, new_sum, new_acc = partial_softmax(queries, every_key, every_value, fresh_valid)
        both_top = jnp.maximum(old_top, new_top)
        old_factor = jnp.exp(old_top - both_top)
        new_factor = jnp.exp(new_top - both_top)
        attended = (old_acc * old_factor[..., None] + new_acc * new_factor[..., None]) / (
            old_sum * old_factor + new_sum * new_factor
        )[..., None]
        attended = attended.astype(jnp.bfloat16).reshape(
            block_steps * total_reqs, kv_local * group_size * HD
        )
        head_term = jnp.dot(attended, proj_out, preferred_element_type=jnp.float32).reshape(
            block_steps, total_reqs, model_width
        )
        stream_full = full_rows.astype(jnp.float32) + lax.psum(
            head_term.astype(jnp.bfloat16), "tp"
        ).astype(jnp.float32)
        mlp_in = rms_scaled(stream_full, mlp_gain).astype(jnp.bfloat16)
        stream = lax.dynamic_slice_in_dim(
            stream_full, tp_rank * local_width, local_width, stream_full.ndim - 1
        )
        mlp_flat = mlp_in.reshape(block_steps * total_reqs, model_width)
        gate_act = jnp.dot(mlp_flat, proj_gate, preferred_element_type=jnp.float32)
        up_act = jnp.dot(mlp_flat, proj_up, preferred_element_type=jnp.float32)
        hidden_act = (jax.nn.silu(gate_act) * up_act).astype(jnp.bfloat16)
        down_term = jnp.dot(hidden_act, proj_down, preferred_element_type=jnp.float32).reshape(
            block_steps, total_reqs, model_width
        )
        result = (
            stream
            + lax.psum_scatter(
                down_term.astype(jnp.bfloat16), "tp", scatter_dimension=2, tiled=True
            ).astype(jnp.float32)
        ).astype(jnp.bfloat16)
        result, key_new, value_new = (result, key_new, value_new)
        collected.append(result)
        prior_keys = prior_keys + [key_new]
        prior_values = prior_values + [value_new]
    output = jnp.concatenate(collected, axis=0)
    return output


def solution(mesh):
    in_specs = (
        P(None, None, "tp"),
        P(),
        P(),
        P(None, "tp"),
        P(None, "tp"),
        P(None, "tp"),
        P("tp", None),
        P(None, "tp"),
        P(None, "tp"),
        P("tp", None),
        P("seq", "tp", None),
        P("seq", "tp", None),
        P("seq", "tp", None),
        P("seq", "tp", None),
        P(),
        P(),
    )
    out_specs = P(None, None, "tp")
    return jax.shard_map(body, mesh=mesh, in_specs=in_specs, out_specs=out_specs, check_vma=False)
```

profile of v0, /device:TPU:0, one launch (start us, length us, event | category | flops | bytes accessed | tf_op | source)
XLA Modules:
  0.0 240.0 jit_solution(4981546146774464908)
XLA Ops:
  7.8 0.8 copy.34
  8.6 6.7 %all_gather.3 = bf16[8,4,2560]{2,0,1:T(8,128)(2,1)S(1)} all-gather(bf16[8,4,640]{2,0,1:T(8,128)(2,1)S(1)} %copy.34), channel_id=1, replica_groups=mesh['seq'=8,'tp'=4] {'tp'}, dimensions={2}, use_global_device_ids=true | all-gather | bytes 204800 | tf_op jit(solution)/shard_map/all_gather | solution.py:108
  15.4 0.6 add_rsqrt_fusion.1
  16.0 0.7 convert_element_type.67
  16.7 5.7 %copy.35 = bf16[2560,640]{0,1:T(8,128)(2,1)} copy(bf16[2560,640]{1,0:T(8,128)(2,1)} %param.19) | data formatting | bytes 6553600 | tf_op args[3]
  22.4 0.7 add_convert_fusion.3
  23.1 0.6 broadcast_compare_fusion
  23.8 0.8 reshape.223
  24.5 0.9 multiply_cosine_fusion
  25.4 3.3 %fusion.18 = f32[8,4,2,4,80]{4,0,3,2,1:T(8,128)S(1)} fusion(bf16[2,4,80,2560,1]{3,2,1,0,4:T(8,128)(2,1)} %bitcast.127, bf16[8,4,2560]{2,0,1:T(8,128)(2,1)S(1)} %all_gather.3, f32[2560]{0:T(1024)S(1)} %convert_element_type.67, f32[8,4]{0,1:T(4,128)} %add_rsqrt_fusion.1), kind=kOutput, calls=%fused_computation.33 | convolution fusion | flops 105185280 | bytes 3532928 | tf_op jit(solution)/shard_map/dot_general | solution.py:113
  28.9 0.9 fusion.72
  29.8 0.9 fusion.71
  30.6 0.6 copy-done.5
  31.2 0.6 pad_maximum_fusion.1
  31.8 37.6 %pmax.7 = f32[8,4,2,4]{0,3,2,1:T(4,128)S(1)} all-reduce(f32[8,4,2,4]{0,3,2,1:T(4,128)} %pad_maximum_fusion.1), channel_id=1, replica_groups=mesh['seq'=8,'tp'=4] {'seq'}, use_global_device_ids=true, to_apply=%region_3.4 | all-reduce | flops 256 | bytes 2048 | tf_op jit(solution)/shard_map/pmax | solution.py:139
  69.5 1.7 fusion.29
  71.1 1.7 fusion.35
  72.9 1.8 convolution_bitcast_fusion.2
  74.7 1.6 reshape.224
  76.3 1.2 convolution_bitcast_fusion.1
  77.5 1.3 maximum_multiply_fusion.1
  78.8 1.5 maximum_multiply_fusion
  80.4 0.6 iota_compare_fusion.1
  81.0 1.6 fusion.22
  82.6 0.7 subtract_convert_fusion.1
  83.3 33.3 %psum.22 = f32[8,4,2,4]{0,3,2,1:T(4,128)S(1)} all-reduce(f32[8,4,2,4]{0,3,2,1:T(4,128)} %get-tuple-element.8), channel_id=1, replica_groups=mesh['seq'=8,'tp'=4] {'seq'}, use_global_device_ids=true, to_apply=%region_8.9 | all-reduce | flops 256 | bytes 2048 | tf_op jit(solution)/shard_map/psum | solution.py:141
  116.6 1.4 fusion.73
  118.0 0.6 copy-done.2
  118.6 0.7 fusion.31
  119.4 28.1 %all-reduce.3.cloned.1.call-done = f32[8,4,2,4,80]{4,0,3,2,1:T(8,128)} async-done(((f32[8,4,2,4,80]{4,0,3,2,1:T(8,128)}), f32[8,4,2,4,80]{4,0,3,2,1:T(8,128)}) %all-reduce.3.cloned.1.call-update) | async-done | bytes 81936 | tf_op jit(solution)/shard_map/psum | solution.py:141
  147.5 2.5 %fusion.7 = bf16[8,4,2,4,80]{4,0,3,2,1:T(8,128)(2,1)} fusion(bf16[2,80,2560,1]{2,1,0,3:T(8,128)(2,1)} %bitcast.142, f32[8,4,2,4,80]{4,0,3,2,1:T(8,128)} %all-reduce.3.cloned.1.call-done, bf16[8,4,2560]{2,0,1:T(8,128)(2,1)S(1)} %all_gather.3, f32[2560]{0:T(1024)} %copy-done.9, f32[8,4]{0,1:T(4,128)} %add_rsqrt_fusion.1, f32[8,4,2,4,8]{0,4,3,2,1:T(8,128)} %copy-done.2, ...), kind=kOutput, calls=%fused_computation.13 | convolution fusion | flops 26983424 | bytes 1128640 | tf_op jit(solution)/shard_map/trkgw,wkrd->trkgd/dot_general | solution.py:56
  150.0 0.9 copy.41
  151.0 1.3 convolution_convert_fusion
  152.4 30.9 %all-reduce.5.cloned.1.call-done = bf16[8,4,2560]{2,0,1:T(8,128)(2,1)} async-done(((bf16[8,4,2560]{2,0,1:T(8,128)(2,1)}), bf16[8,4,2560]{2,0,1:T(8,128)(2,1)}) %all-reduce.5.cloned.1.call-update) | async-done | bytes 163856 | tf_op jit(solution)/shard_map/psum | solution.py:156
  183.3 1.7 convert_add_fusion
  185.0 1.0 multiply_convert_fusion
  186.0 0.7 copy.42
  186.8 1.0 reshape.210
  187.7 3.6 %fusion.74 = f32[32,864]{1,0:T(8,128)S(1)} fusion(bf16[32,2560]{1,0:T(8,128)(2,1)S(1)} %reshape.210, bf16[2560,864]{0,1:T(8,128)(2,1)} %param.23), kind=kOutput, calls=%fused_computation.111 | convolution fusion | flops 141557760 | bytes 4698112 | tf_op jit(solution)/shard_map/dot_general | solution.py:164
  191.3 6.6 %convolution_convert_fusion.1 = bf16[32,2560]{1,0:T(8,128)(2,1)} fusion(bf16[864,2560]{1,0:T(8,128)(2,1)} %param.25, bf16[32,2560]{1,0:T(8,128)(2,1)S(1)} %reshape.210, bf16[2560,864]{0,1:T(8,128)(2,1)} %param.24, f32[32,864]{1,0:T(8,128)S(1)} %fusion.74), kind=kOutput, calls=%fused_computation.1 | convolution fusion | flops 283363328 | bytes 9285632 | tf_op jit(solution)/shard_map/dot_general | solution.py:167
  198.0 1.0 convert_element_type.82
  198.9 2.7 %copy.62 = bf16[8,4,2560]{0,1,2:T(4,128)(2,1)} copy(bf16[8,4,2560]{2,1,0:T(4,128)(2,1)S(1)} %convert_element_type.82) | data formatting | bytes 327680
  201.6 4.3 %reshape.225 = bf16[2560,32]{1,0:T(8,128)(2,1)} reshape(bf16[2560,4,8]{2,1,0:T(4,128)(2,1)} %bitcast.126) | data formatting | bytes 327680
  206.0 22.6 %reduce-scatter.4.cloned.1.call-done = bf16[640,32]{1,0:T(8,128)(2,1)} async-done(((bf16[2560,32]{1,0:T(8,128)(2,1)}), bf16[640,32]{1,0:T(8,128)(2,1)}) %reduce-scatter.4.cloned.1.call-update) | async-done | bytes 40976
  228.6 2.0 reshape.226
  230.6 1.4 copy.63
  232.0 0.9 add_convert_fusion.1
  232.9 0.6 copy.44
  (41 shorter events, 1.2 us)
Async XLA Ops:
  6.5 144.4 %copy-start = (bf16[640,2560]{1,0:T(8,128)(2,1)S(1)}, bf16[640,2560]{1,0:T(8,128)(2,1)}, u32[]{:S(2)}) copy-start(bf16[640,2560]{1,0:T(8,128)(2,1)} %param.22) | copy-start | bytes 9830404
  6.5 15.8 %copy-start.12 = (s32[3]{0:T(128)S(1)}, s32[3]{0:T(128)}, u32[]{:S(2)}) copy-start(s32[3]{0:T(128)} %param.31) | copy-start | bytes 40
  6.5 17.2 %copy-start.8 = (bf16[64,2,240]{2,1,0:T(2,128)(2,1)S(1)}, bf16[64,2,240]{2,1,0:T(2,128)(2,1)}, u32[]{:S(2)}) copy-start(bf16[64,2,240]{2,1,0:T(2,128)(2,1)} %param.28) | copy-start | bytes 184324
  6.5 141.0 %all-reduce.3.cloned.1.call-start = ((), (), s32[]{:S(2)}) async-start(), calls=%async_computation.1 | async-start | bytes 262144 | tf_op jit(solution)/shard_map/psum | solution.py:141
  16.7 12.1 %copy-start.9 = (f32[2560]{0:T(1024)}, f32[2560]{0:T(1024)S(1)}, u32[]{:S(2)}) copy-start(f32[2560]{0:T(1024)S(1)} %convert_element_type.67) | copy-start | bytes 30724
  23.1 6.6 %copy-start.7 = (pred[8,512]{1,0:T(8,128)(4,1)}, pred[8,512]{1,0:T(8,128)(4,1)S(1)}, u32[]{:S(2)}) copy-start(pred[8,512]{1,0:T(8,128)(4,1)S(1)} %iota_compare_fusion) | copy-start | bytes 12292
  24.5 4.3 %copy-start.3 = (bf16[512,2,80]{0,2,1:T(8,128)(2,1)S(1)}, bf16[512,2,80]{0,2,1:T(8,128)(2,1)}, u32[]{:S(2)}) copy-start(bf16[512,2,80]{0,2,1:T(8,128)(2,1)} %param.26) | copy-start | bytes 491524
  24.5 5.2 %copy-start.4 = (bf16[64,2,3,80]{3,2,1,0:T(4,128)(2,1)S(1)}, bf16[64,2,3,80]{3,2,1,0:T(4,128)(2,1)}, u32[]{:S(2)}) copy-start(bf16[64,2,3,80]{3,2,1,0:T(4,128)(2,1)} %reshape.223) | copy-start | bytes 184324
  24.5 5.2 %copy-start.11 = (pred[3,64]{1,0:T(4,128)(4,1)S(1)}, pred[3,64]{1,0:T(4,128)(4,1)}, u32[]{:S(2)}) copy-start(pred[3,64]{1,0:T(4,128)(4,1)} %broadcast_compare_fusion) | copy-start | bytes 580
  28.9 0.9 copy-start.1
  29.7 0.9 copy-start.6
  30.6 0.6 copy-start.5
  80.4 102.9 %all-reduce.5.cloned.1.call-start = ((), (), s32[]{:S(2)}) async-start(), calls=%async_computation.2 | async-start | bytes 327680 | tf_op jit(solution)/shard_map/psum | solution.py:156
  118.0 0.7 copy-start.2
  119.4 33.0 %copy-start.10 = (bf16[2560]{0:T(1024)(128)(2,1)S(1)}, bf16[2560]{0:T(1024)(128)(2,1)}, u32[]{:S(2)}) copy-start(bf16[2560]{0:T(1024)(128)(2,1)} %param.18) | copy-start | bytes 15364
  152.3 76.3 %reduce-scatter.4.cloned.1.call-start = ((), (), s32[]{:S(2)}) async-start(), calls=%async_computation.3 | async-start | bytes 819200
Sparse Core Ops, SparseCore 0:
  80.5 66.9 all-reduce.2
  152.4 30.8 all-reduce.4
  206.1 22.4 reduce-scatter.3
where the time goes:
time: 241 us; the launch traced here: 240 us
  waiting for transfers between devices  81.7 us (34%)
  blocking collectives  77.6 us (32%)
  matrix products  25 us (10%)
  local copies, waits for them, and re-layouts  24.8 us (10%)
  other arithmetic  16.9 us (7%)
  between operations  14 us (6%)
    pmax x1, blocking collectives, body(): global_top = lax.pmax(old_top, 'seq')  37.6 us
    psum x1, blocking collectives, body(): lax.psum((old_sum * rescale, old_acc * rescale[..., None]), 'seq')  33.3 us
    psum x1, waiting for transfers between devices, body(): lax.psum(head_term.astype(jnp.bfloat16), 'tp').astype(jnp.float32)  30.9 us
    psum x1, waiting for transfers between devices, body(): lax.psum((old_sum * rescale, old_acc * rescale[..., None]), 'seq')  28.1 us
    unnamed x4, waiting for transfers between devices  22.7 us
    unnamed x32, local copies, waits for them, and re-layouts  18.2 us
    all_gather x1, blocking collectives, body(): full_rows = lax.all_gather(token_rows, 'tp', axis=2, tiled=True)  6.67 us
    dot_general x1, matrix products, body(): jnp.dot(hidden_act, proj_down, preferred_element_type=jnp.float32)  6.64 us
  transfers between devices with their start and end apart: 3, of which 3 were waited for; matrix products, arithmetic and copies ran while one was open for 2% of the time, Pallas kernels for 0%

commit v1 on v0

v1 whole, which is shorter than its diff:
```python
import functools
import math

import jax
import jax.numpy as jnp
import numpy as np
from jax import lax
from jax.experimental import pallas as pl
from jax.experimental.pallas import tpu as pltpu
from jax.sharding import PartitionSpec as P

HEADS = 32
KV_HEADS = 8
HD = 80
HALF = HD // 2
GROUP = HEADS // KV_HEADS
WIN = 4096
STEPS = 8

EPS = 1e-05
THETA = 10000.0
HIDDEN_SCORE = -1e30
SCALE = 1.0 / math.sqrt(HD)
F32 = jnp.float32
BF16 = jnp.bfloat16
MESH = pl.DeviceIdType.MESH


def up_to(n, unit):
    return -(-n // unit) * unit


def dot(a, b):
    return lax.dot_general(a, b, (((1,), (0,)), ((), ())), preferred_element_type=F32)


def dot_t(a, b):
    return lax.dot_general(a, b, (((1,), (1,)), ((), ())), preferred_element_type=F32)


def pad_rows(v, rows):
    if v.shape[0] == rows:
        return v
    return jnp.concatenate([v, jnp.zeros((rows - v.shape[0], v.shape[1]), v.dtype)], axis=0)


def fold(v, rows):
    parts = []
    for low in range(0, v.shape[1], 128):
        part = v[:, low : min(low + 128, v.shape[1])]
        if part.shape[1] < 128:
            part = jnp.concatenate(
                [part, jnp.zeros((part.shape[0], 128 - part.shape[1]), v.dtype)], axis=1
            )
        parts.append(part)
    return pad_rows(jnp.concatenate(parts, axis=0), rows)


def unfold(v, n, width):
    parts = []
    for k, low in enumerate(range(0, width, 128)):
        parts.append(v[k * n : (k + 1) * n, : min(128, width - low)])
    return jnp.concatenate(parts, axis=1)


def sine_cosine(angle):
    turns = jnp.floor(angle * np.float32(2.0 / math.pi) + 0.5)
    rest = angle - turns * np.float32(1.5703125)
    rest = rest - turns * np.float32(4.8351287841796875e-4)
    rest = rest - turns * np.float32(math.pi / 2 - 1.5703125 - 4.8351287841796875e-4)
    sq = rest * rest
    sine = rest + rest * sq * (
        np.float32(-1.6666654611e-1)
        + sq * (np.float32(8.3321608736e-3) + sq * np.float32(-1.9515295891e-4))
    )
    cosine = 1.0 - 0.5 * sq + sq * sq * (
        np.float32(4.166664568298827e-2)
        + sq * (np.float32(-1.388731625493765e-3) + sq * np.float32(2.443315711809948e-5))
    )
    quarter = turns - 4.0 * jnp.floor(turns * 0.25)
    odd = (quarter == 1.0) | (quarter == 3.0)
    sin_out = jnp.where(odd, cosine, sine)
    cos_out = jnp.where(odd, sine, cosine)
    sin_out = jnp.where(quarter >= 2.0, -sin_out, sin_out)
    cos_out = jnp.where((quarter == 1.0) | (quarter == 2.0), -cos_out, cos_out)
    return sin_out, cos_out


def rope(v, cosine, signed_sine, front):
    ahead = jnp.concatenate([v[:, HALF:], v[:, :HALF]], axis=1)
    behind = jnp.concatenate([v[:, -HALF:], v[:, :-HALF]], axis=1)
    return v * cosine + jnp.where(front, ahead, behind) * signed_sine


def kernel(
    ns, nt, tok, ag, mg, wq, wk, wv, wo, wg, wu, wd, lk, lv, sk, sv, fr, seen, slen, out,
    tok_v, ag_v, mg_v, wq_v, wk_v, wv_v, wo_v, wg_v, wu_v, wd_v, lk_v, lv_v, sk_v, sv_v, fr_v,
    xg, sb, rb, ob, orb, stx, db, drb, frb, local_sem,
    x_send, x_recv, s_send, s_recv, o_send, o_recv, d_send, d_recv, f_send, f_recv,
):
    me_s = lax.axis_index("seq")
    me_t = lax.axis_index("tp")
    steps, reqs, dl = tok.shape
    rows = steps * reqs
    n_tok = rows // ns
    halves = steps // n_tok
    model = wq.shape[0]
    ql = wq.shape[1]
    kl = wk.shape[0]
    heads = ql // HD
    kvl = kl // HD
    long_slots = lk.shape[2]
    short_slots = sk.shape[0]
    fold_rows = frb.shape[1]

    pairs = [
        (tok, tok_v), (ag, ag_v), (fr, fr_v), (wq, wq_v), (wk, wk_v), (wv, wv_v),
        (lk, lk_v), (sk, sk_v), (lv, lv_v), (sv, sv_v), (wo, wo_v), (mg, mg_v),
        (wg, wg_v), (wu, wu_v), (wd, wd_v),
    ]
    copies = {}
    for i, (src, dst) in enumerate(pairs):
        copies[i] = pltpu.make_async_copy(src, dst, local_sem.at[i])
        copies[i].start()

    barrier = pltpu.get_barrier_semaphore()
    for d in range(1, nt):
        pl.semaphore_signal(
            barrier, inc=1, device_id=(me_s, lax.rem(me_t + d, nt)), device_id_type=MESH
        )
    for d in range(1, ns):
        pl.semaphore_signal(
            barrier, inc=1, device_id=(lax.rem(me_s + d, ns), me_t), device_id_type=MESH
        )

    copies[0].wait()
    by_step = [tok_v[t].astype(F32) for t in range(steps)]
    mine = jnp.concatenate(
        [by_step[t][r : r + 1] for r in range(reqs) for t in range(steps)], axis=0
    )
    xg[me_t] = mine.astype(BF16)
    pl.semaphore_wait(barrier, nt - 1 + ns - 1)

    def to_tp(src, dst, send, recv, d):
        return pltpu.make_async_remote_copy(
            src_ref=src, dst_ref=dst, send_sem=send.at[d - 1], recv_sem=recv.at[d - 1],
            device_id=(me_s, lax.rem(me_t + d, nt)), device_id_type=MESH,
        )

    def to_seq(src, dst, send, recv, d):
        return pltpu.make_async_remote_copy(
            src_ref=src, dst_ref=dst, send_sem=send.at[d - 1], recv_sem=recv.at[d - 1],
            device_id=(lax.rem(me_s + d, ns), me_t), device_id_type=MESH,
        )

    x_copies = [to_tp(xg.at[me_t], xg.at[me_t], x_send, x_recv, d) for d in range(1, nt)]
    for copy in x_copies:
        copy.start()

    copies[2].wait()
    row = lax.broadcasted_iota(jnp.int32, (rows, 1), 0)
    req = row // steps
    base = jnp.where(req == 0, seen[0], 0)
    for r in range(1, reqs):
        base = jnp.where(req == r, slen[r - 1], base)
    position = (base + row % steps).astype(F32)
    sine, cosine = sine_cosine(position * fr_v[...])
    lane = lax.broadcasted_iota(jnp.int32, (rows, ql), 1)
    front = lane % HD < HALF
    signed_sine = jnp.where(front, -sine, sine)

    for copy in x_copies:
        copy.wait()
    copies[1].wait()
    pieces = [xg[c].astype(F32) for c in range(nt)]
    square = jnp.zeros((rows, 1), F32)
    for piece in pieces:
        square = square + jnp.sum(piece * piece, axis=-1, keepdims=True)
    inverse = lax.rsqrt(square * np.float32(1.0 / model) + EPS)
    gain = ag_v[...].astype(F32)[None]
    normed = [
        (piece * inverse * gain[:, c * dl : (c + 1) * dl]).astype(BF16)
        for c, piece in enumerate(pieces)
    ]

    def project(parts, weight):
        total = None
        for c, part in enumerate(parts):
            term = dot(part, weight[c * dl : (c + 1) * dl, :])
            total = term if total is None else total + term
        return total

    def project_t(parts, weight):
        total = None
        for c, part in enumerate(parts):
            term = dot_t(part, weight[:, c * dl : (c + 1) * dl])
            total = term if total is None else total + term
        return total

    copies[3].wait()
    query = rope(project(normed, wq_v), cosine, signed_sine, front)
    copies[4].wait()
    key = rope(project_t(normed, wk_v), cosine[:, :kl], signed_sine[:, :kl], front[:, :kl])
    copies[5].wait()
    value = project_t(normed, wv_v)

    for i in (6, 7, 8, 9):
        copies[i].wait()
    short_k = sk_v[...].reshape(short_slots * kvl, sk.shape[2])
    short_v = sv_v[...].reshape(short_slots * kvl, sv.shape[2])
    row_count = heads * steps
    new_count = kvl * steps
    lane128 = lax.broadcasted_iota(jnp.int32, (row_count, 128), 1)
    for r in range(reqs):
        rs = slice(r * steps, (r + 1) * steps)
        q_r = jnp.concatenate(
            [query[rs, h * HD : (h + 1) * HD] for h in range(heads)], axis=0
        ).astype(BF16)
        k_r = jnp.concatenate(
            [key[rs, k * HD : (k + 1) * HD] for k in range(kvl)], axis=0
        ).astype(BF16)
        v_r = jnp.concatenate(
            [value[rs, k * HD : (k + 1) * HD] for k in range(kvl)], axis=0
        ).astype(BF16)
        step_of = lax.broadcasted_iota(jnp.int32, (row_count, 1), 0) % steps
        kv_of = lax.broadcasted_iota(jnp.int32, (row_count, 1), 0) // (steps * GROUP)
        if r == 0:
            col = lax.broadcasted_iota(jnp.int32, (1, long_slots), 1)
            slot = me_s * long_slots + col
            old_mask = ((slot - seen[0]) & (WIN - 1)) > step_of
            span = steps * GROUP
            old_dots = jnp.concatenate(
                [dot(q_r[k * span : (k + 1) * span], lk_v[k]) for k in range(kvl)], axis=0
            )
        else:
            cut = slice((r - 1) * HD, r * HD)
            col = lax.broadcasted_iota(jnp.int32, (1, short_slots * kvl), 1)
            slot = me_s * short_slots + col // kvl
            old_mask = (kv_of == col % kvl) & (slot < slen[r - 1])
            old_dots = dot_t(q_r, short_k[:, cut])
        new_col = lax.broadcasted_iota(jnp.int32, (1, new_count), 1)
        new_mask = (kv_of == new_col // steps) & (new_col % steps <= step_of) & (me_s == 0)
        old_score = jnp.where(old_mask, old_dots * SCALE, HIDDEN_SCORE)
        new_score = jnp.where(new_mask, dot_t(q_r, k_r) * SCALE, HIDDEN_SCORE)
        top = jnp.maximum(
            jnp.max(old_score, axis=-1, keepdims=True), jnp.max(new_score, axis=-1, keepdims=True)
        )
        old_w = jnp.where(old_mask, jnp.exp(old_score - top), 0.0)
        new_w = jnp.where(new_mask, jnp.exp(new_score - top), 0.0)
        total = jnp.sum(old_w, axis=-1, keepdims=True) + jnp.sum(new_w, axis=-1, keepdims=True)
        old_w = old_w.astype(BF16)
        if r == 0:
            acc = jnp.concatenate(
                [dot_t(old_w[k * span : (k + 1) * span], lv_v[k]) for k in range(kvl)], axis=0
            )
        else:
            acc = dot(old_w, short_v[:, cut])
        acc = acc + dot(new_w.astype(BF16), v_r)
        full = jnp.concatenate([acc, jnp.broadcast_to(top, (row_count, 128 - HD))], axis=1)
        full = jnp.where(lane128 == HD + 1, total, full)
        for half in range(halves):
            block = jnp.concatenate(
                [
                    full[h * steps + half * n_tok : h * steps + (half + 1) * n_tok]
                    for h in range(heads)
                ],
                axis=0,
            )
            sb[r * halves + half] = pad_rows(block, sb.shape[1])

    s_copies = [
        to_seq(sb.at[lax.rem(me_s + d, ns)], rb.at[d - 1], s_send, s_recv, d)
        for d in range(1, ns)
    ]
    for copy in s_copies:
        copy.start()
    pick_row = lax.broadcasted_iota(jnp.int32, (8, rows), 0)
    pick_col = lax.broadcasted_iota(jnp.int32, (8, rows), 1)
    pick = jnp.where((pick_col == me_s * n_tok + pick_row) & (pick_row < n_tok), 1.0, 0.0)
    own_x = [dot(pick.astype(BF16), xg[c])[:n_tok] for c in range(nt)]
    for copy in s_copies:
        copy.wait()
    parts = [sb[me_s]] + [rb[d] for d in range(ns - 1)]
    top = parts[0][:, HD : HD + 1]
    for part in parts[1:]:
        top = jnp.maximum(top, part[:, HD : HD + 1])
    merged = jnp.zeros_like(parts[0])
    for part in parts:
        merged = merged + part * jnp.exp(part[:, HD : HD + 1] - top)
    attended = merged[:, :HD] / merged[:, HD + 1 : HD + 2]
    attended = jnp.concatenate(
        [attended[h * n_tok : (h + 1) * n_tok] for h in range(heads)], axis=1
    )
    attended = pad_rows(attended, 8).astype(BF16)

    copies[10].wait()
    head_term = dot(attended, wo_v[...])[:n_tok]
    head_parts = [head_term[:, c * dl : (c + 1) * dl] for c in range(nt)]
    ob[...] = pad_rows(jnp.concatenate(head_parts, axis=0), ob.shape[0]).astype(BF16)
    o_copies = [to_tp(ob, orb.at[d - 1], o_send, o_recv, d) for d in range(1, nt)]
    for copy in o_copies:
        copy.start()
    stream = [a + b for a, b in zip(own_x, head_parts)]
    for copy in o_copies:
        copy.wait()
    for d in range(nt - 1):
        got = orb[d].astype(F32)
        stream = [s + got[c * n_tok : (c + 1) * n_tok] for c, s in enumerate(stream)]

    copies[11].wait()
    square = jnp.zeros((n_tok, 1), F32)
    for piece in stream:
        square = square + jnp.sum(piece * piece, axis=-1, keepdims=True)
    inverse = lax.rsqrt(square * np.float32(1.0 / model) + EPS)
    gain = mg_v[...].astype(F32)[None]
    mlp_in = [
        pad_rows(piece * inverse * gain[:, c * dl : (c + 1) * dl], 8).astype(BF16)
        for c, piece in enumerate(stream)
    ]
    for c, piece in enumerate(stream):
        stx[c] = fold(piece, fold_rows)
    copies[12].wait()
    gate = project_t(mlp_in, wg_v)
    copies[13].wait()
    lift = project_t(mlp_in, wu_v)
    hidden = (gate / (1.0 + jnp.exp(-gate)) * lift).astype(BF16)
    copies[14].wait()
    down = dot(hidden, wd_v[...])[:n_tok]
    for c in range(nt):
        db[c] = fold(down[:, c * dl : (c + 1) * dl], fold_rows).astype(BF16)
    d_copies = [
        to_tp(db.at[lax.rem(me_t + d, nt)], drb.at[d - 1], d_send, d_recv, d)
        for d in range(1, nt)
    ]
    for copy in d_copies:
        copy.start()
    result = stx[me_t] + db[me_t].astype(F32)
    for copy in d_copies:
        copy.wait()
    for d in range(nt - 1):
        result = result + drb[d].astype(F32)
    frb[me_s] = result.astype(BF16)

    f_copies = [to_seq(frb.at[me_s], frb.at[me_s], f_send, f_recv, d) for d in range(1, ns)]
    for copy in f_copies:
        copy.start()
    for copy in f_copies:
        copy.wait()
    out[...] = jnp.concatenate(
        [unfold(frb[j].astype(F32), n_tok, dl) for j in range(ns)], axis=0
    ).astype(BF16)


def body(
    ns, nt, tokens_in, attn_gain, mlp_gain, proj_query, proj_key, proj_value, proj_out,
    proj_gate, proj_up, proj_down, long_keys, long_values, short_keys, short_values,
    long_seen, short_len,
):
    steps, reqs, dl = tokens_in.shape
    model, ql = proj_query.shape
    rows = steps * reqs
    n_tok = rows // ns
    index = (np.arange(ql) % HD) % HALF
    freq = (THETA ** (-2.0 * index.astype(np.float64) / HD)).astype(np.float32)[None]
    operands = (
        tokens_in, attn_gain, mlp_gain, proj_query, proj_key.T, proj_value.T,
        proj_out, proj_gate.T, proj_up.T, proj_down, long_keys.transpose(1, 2, 0),
        long_values.transpose(1, 2, 0), short_keys, short_values, jnp.asarray(freq),
    )
    chunk_rows = up_to((ql // HD) * n_tok, 8)
    fold_rows = up_to(-(-dl // 128) * n_tok, 16)
    out_rows = up_to(nt * n_tok, 16)
    dma = pltpu.SemaphoreType.DMA
    out = pl.pallas_call(
        functools.partial(kernel, ns, nt),
        out_shape=jax.ShapeDtypeStruct((rows, dl), BF16),
        in_specs=[pl.BlockSpec(memory_space=pl.ANY)] * len(operands)
        + [pl.BlockSpec(memory_space=pltpu.SMEM)] * 2,
        out_specs=pl.BlockSpec(memory_space=pltpu.VMEM),
        scratch_shapes=[pltpu.VMEM(a.shape, a.dtype) for a in operands]
        + [
            pltpu.VMEM((nt, rows, dl), BF16),
            pltpu.VMEM((ns, chunk_rows, 128), F32),
            pltpu.VMEM((ns - 1, chunk_rows, 128), F32),
            pltpu.VMEM((out_rows, dl), BF16),
            pltpu.VMEM((nt - 1, out_rows, dl), BF16),
            pltpu.VMEM((nt, fold_rows, 128), F32),
            pltpu.VMEM((nt, fold_rows, 128), BF16),
            pltpu.VMEM((nt - 1, fold_rows, 128), BF16),
            pltpu.VMEM((ns, fold_rows, 128), BF16),
            dma((len(operands),)),
            dma((nt - 1,)), dma((nt - 1,)),
            dma((ns - 1,)), dma((ns - 1,)),
            dma((nt - 1,)), dma((nt - 1,)),
            dma((nt - 1,)), dma((nt - 1,)),
            dma((ns - 1,)), dma((ns - 1,)),
        ],
        compiler_params=pltpu.CompilerParams(
            collective_id=0, has_side_effects=True, vmem_limit_bytes=60 * 1024 * 1024
        ),
    )(*operands, long_seen, short_len)
    return out.reshape(reqs, steps, dl).transpose(1, 0, 2)


def solution(mesh):
    ns, nt = mesh.shape["seq"], mesh.shape["tp"]
    in_specs = (
        P(None, None, "tp"),
        P(),
        P(),
        P(None, "tp"),
        P(None, "tp"),
        P(None, "tp"),
        P("tp", None),
        P(None, "tp"),
        P(None, "tp"),
        P("tp", None),
        P("seq", "tp", None),
        P("seq", "tp", None),
        P("seq", "tp", None),
        P("seq", "tp", None),
        P(),
        P(),
    )
    return jax.shard_map(
        functools.partial(body, ns, nt),
        mesh=mesh,
        in_specs=in_specs,
        out_specs=P(None, None, "tp"),
        check_vma=False,
    )
```

time: 241 us -> 38 us (0.16)
  waiting for transfers between devices: 81.7 us -> 0 us
  blocking collectives: 77.6 us -> 0 us
  Pallas kernels: 0 us -> 35.8 us
  matrix products: 25 us -> 0 us
  local copies, waits for them, and re-layouts: 24.8 us -> 1.41 us
  other arithmetic: 16.9 us -> 0 us
  between operations: 14 us -> 0.66 us
    psum x2 -> x0, waiting for transfers between devices: 59.1 us -> none  [the longest x1 30.9 us: body(): lax.psum(head_term.astype(jnp.bfloat16), 'tp').astype(jnp.float32)]
    pmax x1 -> x0, blocking collectives: 37.6 us -> none  [body(): global_top = lax.pmax(old_top, 'seq')]
    pallas_call x0 -> x1, Pallas kernels: none -> 35.8 us  [body(): pl.pallas_call(functools.partial(kernel, ns, nt), out_shape=jax.ShapeDtyp...]
    psum x1 -> x0, blocking collectives: 33.3 us -> none  [body(): lax.psum((old_sum * rescale, old_acc * rescale[..., None]), 'seq')]
    dot_general x11 -> x0, matrix products: 25 us -> none  [the longest x1 6.64 us: body(): jnp.dot(hidden_act, proj_down, preferred_element_type=jnp.float32)]
    unnamed x4 -> x0, waiting for transfers between devices: 22.7 us -> none
    unnamed x32 -> x0, local copies, waits for them, and re-layouts: 18.2 us -> none
    all_gather x1 -> x0, blocking collectives: 6.67 us -> none  [body(): full_rows = lax.all_gather(token_rows, 'tp', axis=2, tiled=True)]
  transfers between devices with their start and end apart: 3 -> 0, of which waited for: 3 -> 0; matrix products, arithmetic and copies ran while one was open for 2% -> 0% of each run, Pallas kernels for 0% -> 0%
where the time goes in v1:
time: 38 us; the launch traced here: 37.9 us
  Pallas kernels  35.8 us (94%)
  local copies, waits for them, and re-layouts  1.41 us (4%)
  between operations  0.66 us (2%)
    pallas_call x1, Pallas kernels, body(): pl.pallas_call(functools.partial(kernel, ns, nt), out_shape=jax.ShapeDtyp...  35.8 us
    reshape x1, local copies, waits for them, and re-layouts, body(): return out.reshape(reqs, steps, dl).transpose(1, 0, 2)  1.41 us

profile of v1, /device:TPU:0, one launch (start us, length us, event | category | flops | bytes accessed | tf_op | source)
XLA Modules:
  0.0 37.9 jit_solution(17818216948199279445)
XLA Ops:
  0.7 35.8 %shard_map.163 = bf16[32,640]{1,0:T(8,128)(2,1)} custom-call(bf16[8,4,640]{2,1,0:T(4,128)(2,1)} %tok.1, bf16[2560]{0:T(1024)(128)(2,1)} %ag.1, bf16[2560]{0:T(1024)(128)(2,1)} %mg.1, bf16[2560,640]{1,0:T(8,128)(2,1)} %wq.1, bf16[160,2560]{1,0:T(8,128)(2,1)} %bitcast.12, bf16[160,2560]{1,0:T(8,128)(2,1)} %bitcast.13, bf16[640,2560]{1,0:T(8,128)(2,1)} %wo.1, ...), custom_call_target="tpu_custom_call" | custom-call | tf_op jit(solution)/shard_map/pallas_call | solution.py:374
  36.4 1.4 %copy.20 = bf16[4,8,640]{2,0,1:T(4,128)(2,1)} copy(bf16[4,8,640]{2,1,0:T(8,128)(2,1)} %bitcast.16) | data formatting | bytes 81920 | tf_op jit(solution)/shard_map/reshape | solution.py:402

commit v2 on v1

v2 whole, which is shorter than its diff:
```python
import functools
import math

import jax
import jax.numpy as jnp
import numpy as np
from jax import lax
from jax.experimental import pallas as pl
from jax.experimental.pallas import tpu as pltpu
from jax.sharding import PartitionSpec as P

HEADS = 32
KV_HEADS = 8
HD = 80
HALF = HD // 2
GROUP = HEADS // KV_HEADS
WIN = 4096
STEPS = 8

EPS = 1e-05
THETA = 10000.0
HIDDEN_SCORE = -1e30
SCALE = 1.0 / math.sqrt(HD)
F32 = jnp.float32
BF16 = jnp.bfloat16
MESH = pl.DeviceIdType.MESH


def up_to(n, unit):
    return -(-n // unit) * unit


def dot(a, b):
    return lax.dot_general(a, b, (((1,), (0,)), ((), ())), preferred_element_type=F32)


def dot_t(a, b):
    return lax.dot_general(a, b, (((1,), (1,)), ((), ())), preferred_element_type=F32)


def pad_rows(v, rows):
    if v.shape[0] == rows:
        return v
    return jnp.concatenate([v, jnp.zeros((rows - v.shape[0], v.shape[1]), v.dtype)], axis=0)


def iota(shape, axis):
    return lax.broadcasted_iota(jnp.int32, shape, axis)


def one_hot(condition):
    return jnp.where(condition, 1.0, 0.0).astype(BF16)


def sine_cosine(angle):
    turns = jnp.floor(angle * np.float32(2.0 / math.pi) + 0.5)
    rest = angle - turns * np.float32(1.5703125)
    rest = rest - turns * np.float32(4.8351287841796875e-4)
    rest = rest - turns * np.float32(math.pi / 2 - 1.5703125 - 4.8351287841796875e-4)
    sq = rest * rest
    sine = rest + rest * sq * (
        np.float32(-1.6666654611e-1)
        + sq * (np.float32(8.3321608736e-3) + sq * np.float32(-1.9515295891e-4))
    )
    cosine = 1.0 - 0.5 * sq + sq * sq * (
        np.float32(4.166664568298827e-2)
        + sq * (np.float32(-1.388731625493765e-3) + sq * np.float32(2.443315711809948e-5))
    )
    quarter = turns - 4.0 * jnp.floor(turns * 0.25)
    odd = (quarter == 1.0) | (quarter == 3.0)
    sin_out = jnp.where(odd, cosine, sine)
    cos_out = jnp.where(odd, sine, cosine)
    sin_out = jnp.where(quarter >= 2.0, -sin_out, sin_out)
    cos_out = jnp.where((quarter == 1.0) | (quarter == 2.0), -cos_out, cos_out)
    return sin_out, cos_out


def rope(v, cosine, signed_sine, front):
    ahead = jnp.concatenate([v[:, HALF:], v[:, :HALF]], axis=1)
    behind = jnp.concatenate([v[:, -HALF:], v[:, :-HALF]], axis=1)
    return v * cosine + jnp.where(front, ahead, behind) * signed_sine


def kernel(
    ns, nt, tok, ag, mg, wq, wk, wv, wo, wg, wu, wd, lk, lv, sk, sv, fr, seen, slen, out,
    ag_v, mg_v, wq_v, wk_v, wv_v, wo_v, wg_v, wu_v, wd_v, lk_v, lv_v, sk_v, sv_v, fr_v,
    xg, sb, rb, ob, orb, db, drb, fb, local_sem,
    x_send, x_recv, s_send, s_recv, o_send, o_recv, d_send, d_recv, f_send, f_recv,
):
    me_s = lax.axis_index("seq")
    me_t = lax.axis_index("tp")
    steps, reqs, dl = tok.shape
    rows = steps * reqs
    copies_of_step = ns // steps
    my_step = me_s // copies_of_step
    my_twin = lax.rem(me_s, copies_of_step)
    model = wq.shape[0]
    ql = wq.shape[1]
    kl = wk.shape[0]
    heads = ql // HD
    kvl = kl // HD
    long_slots = lk.shape[2]
    short_slots = sk.shape[0]

    barrier = pltpu.get_barrier_semaphore()
    for d in range(1, nt):
        pl.semaphore_signal(
            barrier, inc=1, device_id=(me_s, lax.rem(me_t + d, nt)), device_id_type=MESH
        )
    for d in range(1, ns):
        pl.semaphore_signal(
            barrier, inc=1, device_id=(lax.rem(me_s + d, ns), me_t), device_id_type=MESH
        )

    pairs = [
        (tok, xg.at[me_t]), (ag, ag_v), (fr, fr_v), (wq, wq_v), (wk, wk_v), (wv, wv_v),
        (lk, lk_v), (sk, sk_v), (lv, lv_v), (sv, sv_v), (wo, wo_v), (mg, mg_v),
        (wg, wg_v), (wu, wu_v), (wd, wd_v),
    ]
    copies = []
    for i, (src, dst) in enumerate(pairs):
        copies.append(pltpu.make_async_copy(src, dst, local_sem.at[i]))
        copies[i].start()

    def to_tp(src, dst, send, recv, d):
        return pltpu.make_async_remote_copy(
            src_ref=src, dst_ref=dst, send_sem=send.at[d - 1], recv_sem=recv.at[d - 1],
            device_id=(me_s, lax.rem(me_t + d, nt)), device_id_type=MESH,
        )

    def to_seq(src, dst, send, recv, d, target):
        return pltpu.make_async_remote_copy(
            src_ref=src, dst_ref=dst, send_sem=send.at[d - 1], recv_sem=recv.at[d - 1],
            device_id=(target, me_t), device_id_type=MESH,
        )

    pl.semaphore_wait(barrier, nt - 1 + ns - 1)
    x_copies = [to_tp(tok, xg.at[me_t], x_send, x_recv, d) for d in range(1, nt)]
    for copy in x_copies:
        copy.start()

    copies[2].wait()
    row = iota((rows, 1), 0)
    req = row % reqs
    base = jnp.where(req == 0, seen[0], 0)
    for r in range(1, reqs):
        base = jnp.where(req == r, slen[r - 1], base)
    position = (base + row // reqs).astype(F32)
    sine, cosine = sine_cosine(position * fr_v[...])
    front = iota((rows, ql), 1) % HD < HALF
    signed_sine = jnp.where(front, -sine, sine)
    q_rows, k_rows, m_rows = rows * heads, rows * kvl, reqs * heads
    i = iota((q_rows, 1), 0)
    order_q = one_hot(
        iota((q_rows, q_rows), 1)
        == (i % heads) * rows + (i // heads % steps) * reqs + i // (heads * steps)
    )
    i = iota((k_rows, 1), 0)
    order_k = one_hot(
        iota((k_rows, k_rows), 1)
        == (i // steps % kvl) * rows + (i % steps) * reqs + i // (steps * kvl)
    )
    lane128 = iota((128, 128), 0)
    spread_top = one_hot((lane128 >= HD) & (lane128 < HD + 3))
    spread_heads = one_hot(iota((HD, ql), 1) % HD == iota((HD, ql), 0))
    own_head = iota((m_rows, ql), 1) // HD == iota((m_rows, ql), 0) % heads
    join_heads = one_hot(iota((8, m_rows), 1) // heads == iota((8, m_rows), 0))

    for copy in x_copies:
        copy.wait()
    copies[0].wait()
    copies[1].wait()
    pieces = [xg[c].astype(F32).reshape(rows, dl) for c in range(nt)]
    square = jnp.zeros((rows, 1), F32)
    for piece in pieces:
        square = square + jnp.sum(piece * piece, axis=-1, keepdims=True)
    inverse = lax.rsqrt(square * np.float32(1.0 / model) + EPS)
    gain = ag_v[...].astype(F32)[None]
    normed = [
        (piece * inverse * gain[:, c * dl : (c + 1) * dl]).astype(BF16)
        for c, piece in enumerate(pieces)
    ]

    def project(parts, weight):
        total = None
        for c, part in enumerate(parts):
            term = dot(part, weight[c * dl : (c + 1) * dl, :])
            total = term if total is None else total + term
        return total

    def project_t(parts, weight):
        total = None
        for c, part in enumerate(parts):
            term = dot_t(part, weight[:, c * dl : (c + 1) * dl])
            total = term if total is None else total + term
        return total

    def stack(v, count):
        return jnp.concatenate([v[:, k * HD : (k + 1) * HD] for k in range(count)], axis=0)

    copies[4].wait()
    copies[5].wait()
    copies[3].wait()
    key = rope(project_t(normed, wk_v), cosine[:, :kl], signed_sine[:, :kl], front[:, :kl])
    value = project_t(normed, wv_v)
    query = rope(project(normed, wq_v), cosine, signed_sine, front)
    key = dot(order_k, stack(key, kvl).astype(BF16))
    value = dot(order_k, stack(value, kvl).astype(BF16))
    query = dot(order_q, stack(query, heads).astype(BF16))

    for n in (6, 7, 8, 9):
        copies[n].wait()
    short_k = sk_v[...].reshape(short_slots * kvl, sk.shape[2])
    short_v = sv_v[...].reshape(short_slots * kvl, sv.shape[2])
    row_count = heads * steps
    new_count = kvl * steps
    i = iota((row_count, 1), 0)
    step_of = i // heads
    kv_of = i % heads // GROUP
    new_col = iota((1, new_count), 1)
    new_mask = (kv_of == new_col // steps) & (new_col % steps <= step_of) & (me_s == 0)
    lane = iota((row_count, 128), 1)

    def by_kv(terms):
        total = terms[0]
        for k in range(1, kvl):
            total = jnp.where(kv_of == k, terms[k], total)
        return total

    blocks = []
    for r in range(reqs):
        q_r = query[r * row_count : (r + 1) * row_count].astype(BF16)
        k_r = key[r * new_count : (r + 1) * new_count].astype(BF16)
        v_r = value[r * new_count : (r + 1) * new_count].astype(BF16)
        if r == 0:
            slot = me_s * long_slots + iota((1, long_slots), 1)
            old_mask = ((slot - seen[0]) & (WIN - 1)) > step_of
            old_dots = by_kv([dot(q_r, lk_v[k]) for k in range(kvl)])
        else:
            cut = slice((r - 1) * HD, r * HD)
            col = iota((1, short_slots * kvl), 1)
            slot = me_s * short_slots + col // kvl
            old_mask = (kv_of == col % kvl) & (slot < slen[r - 1])
            old_dots = dot_t(q_r, short_k[:, cut])
        old_score = jnp.where(old_mask, old_dots * SCALE, HIDDEN_SCORE)
        new_score = jnp.where(new_mask, dot_t(q_r, k_r) * SCALE, HIDDEN_SCORE)
        top = jnp.maximum(
            jnp.max(old_score, axis=-1, keepdims=True), jnp.max(new_score, axis=-1, keepdims=True)
        )
        old_w = jnp.where(old_mask, jnp.exp(old_score - top), 0.0)
        new_w = jnp.where(new_mask, jnp.exp(new_score - top), 0.0)
        total = jnp.sum(old_w, axis=-1, keepdims=True) + jnp.sum(new_w, axis=-1, keepdims=True)
        old_w = old_w.astype(BF16)
        if r == 0:
            acc = by_kv([dot_t(old_w, lv_v[k]) for k in range(kvl)])
        else:
            acc = dot(old_w, short_v[:, cut])
        acc = acc + dot(new_w.astype(BF16), v_r)
        full = jnp.concatenate([acc, jnp.zeros((row_count, 128 - HD), F32)], axis=1)
        terms = []
        for number, count in ((top, 3), (total, 2)):
            rest = number
            for _ in range(count):
                term = rest.astype(BF16).astype(F32)
                terms.append(term)
                rest = rest - term
        for n, term in enumerate(terms):
            full = jnp.where(lane == HD + n, term, full)
        blocks.append(full)
    for t in range(steps):
        sb[t] = jnp.concatenate(
            [full[t * heads : (t + 1) * heads] for full in blocks], axis=0
        ).astype(BF16)

    s_copies = []
    for d in range(1, ns):
        target = lax.rem(me_s + d, ns)
        s_copies.append(
            to_seq(sb.at[target // copies_of_step], rb.at[d - 1], s_send, s_recv, d, target)
        )
    for copy in s_copies:
        copy.start()
    stream = [xg[c, my_step].astype(F32) for c in range(nt)]
    for copy in s_copies:
        copy.wait()
    parts = [sb[my_step]] + [rb[d] for d in range(ns - 1)]
    tops = [dot(part, spread_top) for part in parts]
    top = functools.reduce(jnp.maximum, tops)
    merged = jnp.zeros((m_rows, 128), F32)
    for part, part_top in zip(parts, tops):
        merged = merged + part.astype(F32) * jnp.exp(part_top - top)
    attended = merged[:, :HD] / (merged[:, HD + 3 : HD + 4] + merged[:, HD + 4 : HD + 5])
    attended = jnp.where(own_head, dot(attended.astype(BF16), spread_heads), 0.0).astype(BF16)
    attended = dot(join_heads, attended).astype(BF16)

    copies[10].wait()
    head_term = dot(attended, wo_v[...])[:reqs]
    head_parts = [head_term[:, c * dl : (c + 1) * dl] for c in range(nt)]
    ob[...] = jnp.concatenate(head_parts, axis=0).astype(BF16)
    o_copies = [to_tp(ob, orb.at[d - 1], o_send, o_recv, d) for d in range(1, nt)]
    for copy in o_copies:
        copy.start()
    stream = [a + b for a, b in zip(stream, head_parts)]
    copies[11].wait()
    gain = mg_v[...].astype(F32)[None]
    for copy in o_copies:
        copy.wait()
    got = orb[0].astype(F32)
    for d in range(1, nt - 1):
        got = got + orb[d].astype(F32)
    stream = [s + got[c * reqs : (c + 1) * reqs] for c, s in enumerate(stream)]
    square = jnp.zeros((reqs, 1), F32)
    for piece in stream:
        square = square + jnp.sum(piece * piece, axis=-1, keepdims=True)
    inverse = lax.rsqrt(square * np.float32(1.0 / model) + EPS)
    mlp_in = [
        pad_rows(piece * inverse * gain[:, c * dl : (c + 1) * dl], 8).astype(BF16)
        for c, piece in enumerate(stream)
    ]
    copies[12].wait()
    gate = project_t(mlp_in, wg_v)
    copies[13].wait()
    lift = project_t(mlp_in, wu_v)
    hidden = (gate / (1.0 + jnp.exp(-gate)) * lift).astype(BF16)
    copies[14].wait()
    down = dot(hidden, wd_v[...])[:reqs]
    result = jnp.zeros((reqs, dl), F32)
    for c in range(nt):
        piece = down[:, c * dl : (c + 1) * dl]
        db[c] = piece.astype(BF16)
        result = result + jnp.where(me_t == c, stream[c] + piece, 0.0)
    d_copies = [
        to_tp(db.at[lax.rem(me_t + d, nt)], drb.at[d - 1], d_send, d_recv, d)
        for d in range(1, nt)
    ]
    for copy in d_copies:
        copy.start()
    for copy in d_copies:
        copy.wait()
    for d in range(nt - 1):
        result = result + drb[d].astype(F32)
    fb[...] = result.astype(BF16)

    f_copies = []
    for d in range(1, steps):
        target = lax.rem(my_step + d, steps) * copies_of_step + my_twin
        f_copies.append(to_seq(fb, out.at[my_step], f_send, f_recv, d, target))
    for copy in f_copies:
        copy.start()
    own = pltpu.make_async_copy(fb, out.at[my_step], local_sem.at[len(pairs)])
    own.start()
    for copy in f_copies:
        copy.wait()
    own.wait()


def body(
    ns, nt, tokens_in, attn_gain, mlp_gain, proj_query, proj_key, proj_value, proj_out,
    proj_gate, proj_up, proj_down, long_keys, long_values, short_keys, short_values,
    long_seen, short_len,
):
    steps, reqs, dl = tokens_in.shape
    ql = proj_query.shape[1]
    rows = steps * reqs
    m_rows = reqs * (ql // HD)
    index = (np.arange(ql) % HD) % HALF
    freq = (THETA ** (-2.0 * index.astype(np.float64) / HD)).astype(np.float32)[None]
    operands = (
        tokens_in, attn_gain, mlp_gain, proj_query, proj_key.T, proj_value.T,
        proj_out, proj_gate.T, proj_up.T, proj_down, long_keys.transpose(1, 2, 0),
        long_values.transpose(1, 2, 0), short_keys, short_values, jnp.asarray(freq),
    )
    dma = pltpu.SemaphoreType.DMA
    return pl.pallas_call(
        functools.partial(kernel, ns, nt),
        out_shape=jax.ShapeDtypeStruct(tokens_in.shape, BF16),
        in_specs=[pl.BlockSpec(memory_space=pl.ANY)] * len(operands)
        + [pl.BlockSpec(memory_space=pltpu.SMEM)] * 2,
        out_specs=pl.BlockSpec(memory_space=pl.ANY),
        scratch_shapes=[pltpu.VMEM(a.shape, a.dtype) for a in operands[1:]]
        + [
            pltpu.VMEM((nt, steps, reqs, dl), BF16),
            pltpu.VMEM((steps, m_rows, 128), BF16),
            pltpu.VMEM((ns - 1, m_rows, 128), BF16),
            pltpu.VMEM((nt * reqs, dl), BF16),
            pltpu.VMEM((nt - 1, nt * reqs, dl), BF16),
            pltpu.VMEM((nt, reqs, dl), BF16),
            pltpu.VMEM((nt - 1, reqs, dl), BF16),
            pltpu.VMEM((reqs, dl), BF16),
            dma((len(operands) + 1,)),
            dma((nt - 1,)), dma((nt - 1,)),
            dma((ns - 1,)), dma((ns - 1,)),
            dma((nt - 1,)), dma((nt - 1,)),
            dma((nt - 1,)), dma((nt - 1,)),
            dma((steps - 1,)), dma((steps - 1,)),
        ],
        compiler_params=pltpu.CompilerParams(
            collective_id=0, has_side_effects=True, vmem_limit_bytes=60 * 1024 * 1024
        ),
    )(*operands, long_seen, short_len)


def solution(mesh):
    ns, nt = mesh.shape["seq"], mesh.shape["tp"]
    in_specs = (
        P(None, None, "tp"),
        P(),
        P(),
        P(None, "tp"),
        P(None, "tp"),
        P(None, "tp"),
        P("tp", None),
        P(None, "tp"),
        P(None, "tp"),
        P("tp", None),
        P("seq", "tp", None),
        P("seq", "tp", None),
        P("seq", "tp", None),
        P("seq", "tp", None),
        P(),
        P(),
    )
    return jax.shard_map(
        functools.partial(body, ns, nt),
        mesh=mesh,
        in_specs=in_specs,
        out_specs=P(None, None, "tp"),
        check_vma=False,
    )
```

time: 38 us -> 36.4 us (0.958)
  Pallas kernels: 35.8 us -> 34.2 us
    pallas_call x1, Pallas kernels: 35.8 us -> 34.2 us  [body(): pl.pallas_call(functools.partial(kernel, ns, nt), out_shape=jax.ShapeDtyp...]
    reshape x1 -> x0, local copies, waits for them, and re-layouts: 1.41 us -> none  [body(): return out.reshape(reqs, steps, dl).transpose(1, 0, 2)]
    unnamed x0 -> x1, local copies, waits for them, and re-layouts: none -> 1.41 us
where the time goes in v2:
time: 36.4 us; the launch traced here: 36.2 us
  Pallas kernels  34.2 us (94%)
  local copies, waits for them, and re-layouts  1.41 us (4%)
  between operations  0.66 us (2%)
    pallas_call x1, Pallas kernels, body(): pl.pallas_call(functools.partial(kernel, ns, nt), out_shape=jax.ShapeDtyp...  34.2 us
    unnamed x1, local copies, waits for them, and re-layouts  1.41 us

profile of v2, /device:TPU:0, one launch (start us, length us, event | category | flops | bytes accessed | tf_op | source)
XLA Modules:
  0.0 36.2 jit_solution(13338523721825180202)
XLA Ops:
  0.7 34.2 %shard_map.163 = bf16[8,4,640]{2,1,0:T(4,128)(2,1)} custom-call(bf16[8,4,640]{2,1,0:T(4,128)(2,1)} %tok.1, bf16[2560]{0:T(1024)(128)(2,1)} %ag.1, bf16[2560]{0:T(1024)(128)(2,1)} %mg.1, bf16[2560,640]{1,0:T(8,128)(2,1)} %wq.1, bf16[160,2560]{1,0:T(8,128)(2,1)} %bitcast.8, bf16[160,2560]{1,0:T(8,128)(2,1)} %bitcast.9, bf16[640,2560]{1,0:T(8,128)(2,1)} %wo.1, ...), custom_call_target="tpu_custom_call" | custom-call | tf_op jit(solution)/shard_map/pallas_call | solution.py:374
  34.8 1.4 %copy.20 = bf16[8,4,640]{2,1,0:T(4,128)(2,1)} copy(bf16[8,4,640]{2,1,0:T(4,128)(2,1)} %shard_map.163) | data formatting | bytes 81920

commit v3 on v2

--- a/solution.py
+++ b/solution.py
@@ -24,10 +24,6 @@
 F32 = jnp.float32
 BF16 = jnp.bfloat16
 MESH = pl.DeviceIdType.MESH
-
-
-def up_to(n, unit):
-    return -(-n // unit) * unit
 
 
 def dot(a, b):
@@ -112,15 +108,28 @@
             barrier, inc=1, device_id=(lax.rem(me_s + d, ns), me_t), device_id_type=MESH
         )
 
-    pairs = [
-        (tok, xg.at[me_t]), (ag, ag_v), (fr, fr_v), (wq, wq_v), (wk, wk_v), (wv, wv_v),
-        (lk, lk_v), (sk, sk_v), (lv, lv_v), (sv, sv_v), (wo, wo_v), (mg, mg_v),
-        (wg, wg_v), (wu, wu_v), (wd, wd_v),
-    ]
-    copies = []
-    for i, (src, dst) in enumerate(pairs):
-        copies.append(pltpu.make_async_copy(src, dst, local_sem.at[i]))
-        copies[i].start()
+    def load(n, src, dst):
+        return pltpu.make_async_copy(src, dst, local_sem.at[n])
+
+    first = [
+        load(0, wk, wk_v), load(1, wv, wv_v), load(2, fr, fr_v), load(3, ag, ag_v),
+        load(4, tok, xg.at[me_t]),
+    ]
+    first += [
+        load(5 + c, wq.at[pl.ds(c * dl, dl)], wq_v.at[pl.ds(c * dl, dl)]) for c in range(nt)
+    ]
+    cached = [
+        load(5 + nt + n, src, dst)
+        for n, (src, dst) in enumerate([(lk, lk_v), (sk, sk_v), (lv, lv_v), (sv, sv_v)])
+    ]
+    later = [
+        load(9 + nt + n, src, dst)
+        for n, (src, dst) in enumerate(
+            [(mg, mg_v), (wo, wo_v), (wg, wg_v), (wu, wu_v), (wd, wd_v)]
+        )
+    ]
+    for copy in first + cached:
+        copy.start()
 
     def to_tp(src, dst, send, recv, d):
         return pltpu.make_async_remote_copy(
@@ -139,7 +148,7 @@
     for copy in x_copies:
         copy.start()
 
-    copies[2].wait()
+    first[2].wait()
     row = iota((rows, 1), 0)
     req = row % reqs
     base = jnp.where(req == 0, seen[0], 0)
@@ -166,10 +175,13 @@
     own_head = iota((m_rows, ql), 1) // HD == iota((m_rows, ql), 0) % heads
     join_heads = one_hot(iota((8, m_rows), 1) // heads == iota((8, m_rows), 0))
 
+    for n, copy in enumerate(first + cached):
+        if n != 2:
+            copy.wait()
+    for copy in later:
+        copy.start()
     for copy in x_copies:
         copy.wait()
-    copies[0].wait()
-    copies[1].wait()
     pieces = [xg[c].astype(F32).reshape(rows, dl) for c in range(nt)]
     square = jnp.zeros((rows, 1), F32)
     for piece in pieces:
@@ -198,9 +210,6 @@
     def stack(v, count):
         return jnp.concatenate([v[:, k * HD : (k + 1) * HD] for k in range(count)], axis=0)
 
-    copies[4].wait()
-    copies[5].wait()
-    copies[3].wait()
     key = rope(project_t(normed, wk_v), cosine[:, :kl], signed_sine[:, :kl], front[:, :kl])
     value = project_t(normed, wv_v)
     query = rope(project(normed, wq_v), cosine, signed_sine, front)
@@ -208,8 +217,6 @@
     value = dot(order_k, stack(value, kvl).astype(BF16))
     query = dot(order_q, stack(query, heads).astype(BF16))
 
-    for n in (6, 7, 8, 9):
-        copies[n].wait()
     short_k = sk_v[...].reshape(short_slots * kvl, sk.shape[2])
     short_v = sv_v[...].reshape(short_slots * kvl, sv.shape[2])
     row_count = heads * steps
@@ -293,7 +300,7 @@
     attended = jnp.where(own_head, dot(attended.astype(BF16), spread_heads), 0.0).astype(BF16)
     attended = dot(join_heads, attended).astype(BF16)
 
-    copies[10].wait()
+    later[1].wait()
     head_term = dot(attended, wo_v[...])[:reqs]
     head_parts = [head_term[:, c * dl : (c + 1) * dl] for c in range(nt)]
     ob[...] = jnp.concatenate(head_parts, axis=0).astype(BF16)
@@ -301,7 +308,7 @@
     for copy in o_copies:
         copy.start()
     stream = [a + b for a, b in zip(stream, head_parts)]
-    copies[11].wait()
+    later[0].wait()
     gain = mg_v[...].astype(F32)[None]
     for copy in o_copies:
         copy.wait()
@@ -317,12 +324,12 @@
         pad_rows(piece * inverse * gain[:, c * dl : (c + 1) * dl], 8).astype(BF16)
         for c, piece in enumerate(stream)
     ]
-    copies[12].wait()
+    later[2].wait()
     gate = project_t(mlp_in, wg_v)
-    copies[13].wait()
+    later[3].wait()
     lift = project_t(mlp_in, wu_v)
     hidden = (gate / (1.0 + jnp.exp(-gate)) * lift).astype(BF16)
-    copies[14].wait()
+    later[4].wait()
     down = dot(hidden, wd_v[...])[:reqs]
     result = jnp.zeros((reqs, dl), F32)
     for c in range(nt):
@@ -347,7 +354,7 @@
         f_copies.append(to_seq(fb, out.at[my_step], f_send, f_recv, d, target))
     for copy in f_copies:
         copy.start()
-    own = pltpu.make_async_copy(fb, out.at[my_step], local_sem.at[len(pairs)])
+    own = pltpu.make_async_copy(fb, out.at[my_step], local_sem.at[14 + nt])
     own.start()
     for copy in f_copies:
         copy.wait()
@@ -387,7 +394,7 @@
             pltpu.VMEM((nt, reqs, dl), BF16),
             pltpu.VMEM((nt - 1, reqs, dl), BF16),
             pltpu.VMEM((reqs, dl), BF16),
-            dma((len(operands) + 1,)),
+            dma((15 + nt,)),
             dma((nt - 1,)), dma((nt - 1,)),
             dma((ns - 1,)), dma((ns - 1,)),
             dma((nt - 1,)), dma((nt - 1,)),

time: 36.4 us -> 36.2 us (level)
  no operation moved by 1% of the time
where the time goes in v3:
time: 36.2 us; the launch traced here: 36.1 us
  Pallas kernels  34 us (94%)
  local copies, waits for them, and re-layouts  1.41 us (4%)
  between operations  0.66 us (2%)
    pallas_call x1, Pallas kernels, body(): pl.pallas_call(functools.partial(kernel, ns, nt), out_shape=jax.ShapeDtyp...  34 us
    unnamed x1, local copies, waits for them, and re-layouts  1.41 us

profile of v3, /device:TPU:0, one launch (start us, length us, event | category | flops | bytes accessed | tf_op | source)
XLA Modules:
  0.0 36.1 jit_solution(18403385934947474717)
XLA Ops:
  0.7 34.0 %shard_map.163 = bf16[8,4,640]{2,1,0:T(4,128)(2,1)} custom-call(bf16[8,4,640]{2,1,0:T(4,128)(2,1)} %tok.1, bf16[2560]{0:T(1024)(128)(2,1)} %ag.1, bf16[2560]{0:T(1024)(128)(2,1)} %mg.1, bf16[2560,640]{1,0:T(8,128)(2,1)} %wq.1, bf16[160,2560]{1,0:T(8,128)(2,1)} %bitcast.8, bf16[160,2560]{1,0:T(8,128)(2,1)} %bitcast.9, bf16[640,2560]{1,0:T(8,128)(2,1)} %wo.1, ...), custom_call_target="tpu_custom_call" | custom-call | tf_op jit(solution)/shard_map/pallas_call | solution.py:381
  34.7 1.4 %copy.20 = bf16[8,4,640]{2,1,0:T(4,128)(2,1)} copy(bf16[8,4,640]{2,1,0:T(4,128)(2,1)} %shard_map.163) | data formatting | bytes 81920

commit v4 on v3

--- a/solution.py
+++ b/solution.py
@@ -90,6 +90,11 @@
     copies_of_step = ns // steps
     my_step = me_s // copies_of_step
     my_twin = lax.rem(me_s, copies_of_step)
+    half = lax.rem(my_step, 2)
+    mate_step = my_step + 1 - 2 * half
+    mate = mate_step * copies_of_step + my_twin
+    ff, share = wd.shape[0], wd_v.shape[0]
+    low = pl.multiple_of(half * (ff - share), 16)
     model = wq.shape[0]
     ql = wq.shape[1]
     kl = wk.shape[0]
@@ -108,6 +113,11 @@
             barrier, inc=1, device_id=(lax.rem(me_s + d, ns), me_t), device_id_type=MESH
         )
 
+    for d in range(1, nt):
+        pl.semaphore_signal(
+            barrier, inc=1, device_id=(mate, lax.rem(me_t + d, nt)), device_id_type=MESH
+        )
+
     def load(n, src, dst):
         return pltpu.make_async_copy(src, dst, local_sem.at[n])
 
@@ -125,7 +135,13 @@
     later = [
         load(9 + nt + n, src, dst)
         for n, (src, dst) in enumerate(
-            [(mg, mg_v), (wo, wo_v), (wg, wg_v), (wu, wu_v), (wd, wd_v)]
+            [
+                (mg, mg_v),
+                (wo, wo_v),
+                (wg.at[pl.ds(low, share)], wg_v),
+                (wu.at[pl.ds(low, share)], wu_v),
+                (wd.at[pl.ds(low, share)], wd_v),
+            ]
         )
     ]
     for copy in first + cached:
@@ -137,13 +153,20 @@
             device_id=(me_s, lax.rem(me_t + d, nt)), device_id_type=MESH,
         )
 
+    def to_pair(src, dst, send, recv, e):
+        return pltpu.make_async_remote_copy(
+            src_ref=src, dst_ref=dst, send_sem=send.at[e - 1], recv_sem=recv.at[e - 1],
+            device_id=(me_s if e < nt else mate, lax.rem(me_t + e % nt, nt)),
+            device_id_type=MESH,
+        )
+
     def to_seq(src, dst, send, recv, d, target):
         return pltpu.make_async_remote_copy(
             src_ref=src, dst_ref=dst, send_sem=send.at[d - 1], recv_sem=recv.at[d - 1],
             device_id=(target, me_t), device_id_type=MESH,
         )
 
-    pl.semaphore_wait(barrier, nt - 1 + ns - 1)
+    pl.semaphore_wait(barrier, nt - 1 + ns - 1 + nt - 1)
     x_copies = [to_tp(tok, xg.at[me_t], x_send, x_recv, d) for d in range(1, nt)]
     for copy in x_copies:
         copy.start()
@@ -288,6 +311,7 @@
     for copy in s_copies:
         copy.start()
     stream = [xg[c, my_step].astype(F32) for c in range(nt)]
+    mate_stream = [xg[c, mate_step].astype(F32) for c in range(nt)]
     for copy in s_copies:
         copy.wait()
     parts = [sb[my_step]] + [rb[d] for d in range(ns - 1)]
@@ -304,7 +328,7 @@
     head_term = dot(attended, wo_v[...])[:reqs]
     head_parts = [head_term[:, c * dl : (c + 1) * dl] for c in range(nt)]
     ob[...] = jnp.concatenate(head_parts, axis=0).astype(BF16)
-    o_copies = [to_tp(ob, orb.at[d - 1], o_send, o_recv, d) for d in range(1, nt)]
+    o_copies = [to_pair(ob, orb.at[e - 1], o_send, o_recv, e) for e in range(1, 2 * nt)]
     for copy in o_copies:
         copy.start()
     stream = [a + b for a, b in zip(stream, head_parts)]
@@ -312,40 +336,52 @@
     gain = mg_v[...].astype(F32)[None]
     for copy in o_copies:
         copy.wait()
-    got = orb[0].astype(F32)
-    for d in range(1, nt - 1):
-        got = got + orb[d].astype(F32)
-    stream = [s + got[c * reqs : (c + 1) * reqs] for c, s in enumerate(stream)]
-    square = jnp.zeros((reqs, 1), F32)
-    for piece in stream:
+
+    def summed(slots):
+        got = orb[slots[0]].astype(F32)
+        for slot in slots[1:]:
+            got = got + orb[slot].astype(F32)
+        return [got[c * reqs : (c + 1) * reqs] for c in range(nt)]
+
+    stream = [a + b for a, b in zip(stream, summed(range(nt - 1)))]
+    mate_stream = [a + b for a, b in zip(mate_stream, summed(range(nt - 1, 2 * nt - 1)))]
+    both = [jnp.concatenate([a, b], axis=0) for a, b in zip(stream, mate_stream)]
+    square = jnp.zeros((2 * reqs, 1), F32)
+    for piece in both:
         square = square + jnp.sum(piece * piece, axis=-1, keepdims=True)
     inverse = lax.rsqrt(square * np.float32(1.0 / model) + EPS)
     mlp_in = [
-        pad_rows(piece * inverse * gain[:, c * dl : (c + 1) * dl], 8).astype(BF16)
-        for c, piece in enumerate(stream)
+        (piece * inverse * gain[:, c * dl : (c + 1) * dl]).astype(BF16)
+        for c, piece in enumerate(both)
     ]
     later[2].wait()
     gate = project_t(mlp_in, wg_v)
     later[3].wait()
     lift = project_t(mlp_in, wu_v)
-    hidden = (gate / (1.0 + jnp.exp(-gate)) * lift).astype(BF16)
+    hidden = gate / (1.0 + jnp.exp(-gate)) * lift
+    if 2 * share > ff:
+        shared = (iota((1, share), 1) < 2 * share - ff) & (half == 1)
+        hidden = jnp.where(shared, 0.0, hidden)
     later[4].wait()
-    down = dot(hidden, wd_v[...])[:reqs]
+    down = dot(hidden.astype(BF16), wd_v[...])
     result = jnp.zeros((reqs, dl), F32)
     for c in range(nt):
         piece = down[:, c * dl : (c + 1) * dl]
-        db[c] = piece.astype(BF16)
-        result = result + jnp.where(me_t == c, stream[c] + piece, 0.0)
+        db[0, c] = piece[:reqs].astype(BF16)
+        db[1, c] = piece[reqs:].astype(BF16)
+        result = result + jnp.where(me_t == c, stream[c] + piece[:reqs], 0.0)
     d_copies = [
-        to_tp(db.at[lax.rem(me_t + d, nt)], drb.at[d - 1], d_send, d_recv, d)
-        for d in range(1, nt)
+        to_pair(
+            db.at[e // nt, lax.rem(me_t + e % nt, nt)], drb.at[e - 1], d_send, d_recv, e
+        )
+        for e in range(1, 2 * nt)
     ]
     for copy in d_copies:
         copy.start()
     for copy in d_copies:
         copy.wait()
-    for d in range(nt - 1):
-        result = result + drb[d].astype(F32)
+    for e in range(2 * nt - 1):
+        result = result + drb[e].astype(F32)
     fb[...] = result.astype(BF16)
 
     f_copies = []
@@ -377,6 +413,8 @@
         proj_out, proj_gate.T, proj_up.T, proj_down, long_keys.transpose(1, 2, 0),
         long_values.transpose(1, 2, 0), short_keys, short_values, jnp.asarray(freq),
     )
+    ff = proj_down.shape[0]
+    share = -(-ff // 32) * 16
     dma = pltpu.SemaphoreType.DMA
     return pl.pallas_call(
         functools.partial(kernel, ns, nt),
@@ -384,21 +422,24 @@
         in_specs=[pl.BlockSpec(memory_space=pl.ANY)] * len(operands)
         + [pl.BlockSpec(memory_space=pltpu.SMEM)] * 2,
         out_specs=pl.BlockSpec(memory_space=pl.ANY),
-        scratch_shapes=[pltpu.VMEM(a.shape, a.dtype) for a in operands[1:]]
+        scratch_shapes=[
+            pltpu.VMEM((share if a.shape[0] == ff else a.shape[0],) + a.shape[1:], a.dtype)
+            for a in operands[1:]
+        ]
         + [
             pltpu.VMEM((nt, steps, reqs, dl), BF16),
             pltpu.VMEM((steps, m_rows, 128), BF16),
             pltpu.VMEM((ns - 1, m_rows, 128), BF16),
             pltpu.VMEM((nt * reqs, dl), BF16),
-            pltpu.VMEM((nt - 1, nt * reqs, dl), BF16),
-            pltpu.VMEM((nt, reqs, dl), BF16),
-            pltpu.VMEM((nt - 1, reqs, dl), BF16),
+            pltpu.VMEM((2 * nt - 1, nt * reqs, dl), BF16),
+            pltpu.VMEM((2, nt, reqs, dl), BF16),
+            pltpu.VMEM((2 * nt - 1, reqs, dl), BF16),
             pltpu.VMEM((reqs, dl), BF16),
             dma((15 + nt,)),
             dma((nt - 1,)), dma((nt - 1,)),
             dma((ns - 1,)), dma((ns - 1,)),
-            dma((nt - 1,)), dma((nt - 1,)),
-            dma((nt - 1,)), dma((nt - 1,)),
+            dma((2 * nt - 1,)), dma((2 * nt - 1,)),
+            dma((2 * nt - 1,)), dma((2 * nt - 1,)),
             dma((steps - 1,)), dma((steps - 1,)),
         ],
         compiler_params=pltpu.CompilerParams(

time: 36.2 us -> 34.9 us (0.964)
  Pallas kernels: 34 us -> 32.7 us
    pallas_call x1, Pallas kernels: 34 us -> 32.7 us  [body(): pl.pallas_call(functools.partial(kernel, ns, nt), out_shape=jax.ShapeDtyp...]
where the time goes in v4:
time: 34.9 us; the launch traced here: 34.8 us
  Pallas kernels  32.7 us (94%)
  local copies, waits for them, and re-layouts  1.41 us (4%)
  between operations  0.66 us (2%)
    pallas_call x1, Pallas kernels, body(): pl.pallas_call(functools.partial(kernel, ns, nt), out_shape=jax.ShapeDtyp...  32.7 us
    unnamed x1, local copies, waits for them, and re-layouts  1.41 us

profile of v4, /device:TPU:0, one launch (start us, length us, event | category | flops | bytes accessed | tf_op | source)
XLA Modules:
  0.0 34.8 jit_solution(7678057278497708483)
XLA Ops:
  0.7 32.7 %shard_map.163 = bf16[8,4,640]{2,1,0:T(4,128)(2,1)} custom-call(bf16[8,4,640]{2,1,0:T(4,128)(2,1)} %tok.1, bf16[2560]{0:T(1024)(128)(2,1)} %ag.1, bf16[2560]{0:T(1024)(128)(2,1)} %mg.1, bf16[2560,640]{1,0:T(8,128)(2,1)} %wq.1, bf16[160,2560]{1,0:T(8,128)(2,1)} %bitcast.8, bf16[160,2560]{1,0:T(8,128)(2,1)} %bitcast.9, bf16[640,2560]{1,0:T(8,128)(2,1)} %wo.1, ...), custom_call_target="tpu_custom_call" | custom-call | tf_op jit(solution)/shard_map/pallas_call | solution.py:419
  33.4 1.4 %copy.20 = bf16[8,4,640]{2,1,0:T(4,128)(2,1)} copy(bf16[8,4,640]{2,1,0:T(4,128)(2,1)} %shard_map.163) | data formatting | bytes 81920

commit v5 on v4

--- a/solution.py
+++ b/solution.py
@@ -42,6 +42,15 @@
 
 def iota(shape, axis):
     return lax.broadcasted_iota(jnp.int32, shape, axis)
+
+
+def flip(index, mask):
+    bit = 1
+    while bit <= mask:
+        if mask & bit:
+            index = index + bit - 2 * bit * (index // bit % 2)
+        bit *= 2
+    return index
 
 
 def one_hot(condition):
@@ -147,12 +156,6 @@
     for copy in first + cached:
         copy.start()
 
-    def to_tp(src, dst, send, recv, d):
-        return pltpu.make_async_remote_copy(
-            src_ref=src, dst_ref=dst, send_sem=send.at[d - 1], recv_sem=recv.at[d - 1],
-            device_id=(me_s, lax.rem(me_t + d, nt)), device_id_type=MESH,
-        )
-
     def to_pair(src, dst, send, recv, e):
         return pltpu.make_async_remote_copy(
             src_ref=src, dst_ref=dst, send_sem=send.at[e - 1], recv_sem=recv.at[e - 1],
@@ -167,7 +170,13 @@
         )
 
     pl.semaphore_wait(barrier, nt - 1 + ns - 1 + nt - 1)
-    x_copies = [to_tp(tok, xg.at[me_t], x_send, x_recv, d) for d in range(1, nt)]
+    x_copies = [
+        pltpu.make_async_remote_copy(
+            src_ref=tok, dst_ref=xg.at[me_t], send_sem=x_send.at[d - 1],
+            recv_sem=x_recv.at[d - 1], device_id=(me_s, flip(me_t, d)), device_id_type=MESH,
+        )
+        for d in range(1, nt)
+    ]
     for copy in x_copies:
         copy.start()
 
@@ -203,25 +212,34 @@
             copy.wait()
     for copy in later:
         copy.start()
-    for copy in x_copies:
-        copy.wait()
-    pieces = [xg[c].astype(F32).reshape(rows, dl) for c in range(nt)]
+    gain = ag_v[...].astype(F32)[None]
+    gains = [gain[:, c * dl : (c + 1) * dl] for c in range(nt)]
     square = jnp.zeros((rows, 1), F32)
-    for piece in pieces:
+    query = jnp.zeros((rows, ql), F32)
+    key = jnp.zeros((rows, kl), F32)
+    value = jnp.zeros((rows, kl), F32)
+    in_turn = dl % 128 == 0
+    if not in_turn:
+        for copy in x_copies:
+            copy.wait()
+    for d in range(nt):
+        if in_turn:
+            if d:
+                x_copies[d - 1].wait()
+            c = flip(me_t, d)
+            here = pl.ds(pl.multiple_of(c * dl, 128), dl)
+            gain = gains[0]
+            for n in range(1, nt):
+                gain = jnp.where(c == n, gains[n], gain)
+        else:
+            c, here, gain = d, pl.ds(d * dl, dl), gains[d]
+        piece = xg[c].astype(F32).reshape(rows, dl)
         square = square + jnp.sum(piece * piece, axis=-1, keepdims=True)
+        piece = (piece * gain).astype(BF16)
+        key = key + dot_t(piece, wk_v[:, here])
+        value = value + dot_t(piece, wv_v[:, here])
+        query = query + dot(piece, wq_v[here, :])
     inverse = lax.rsqrt(square * np.float32(1.0 / model) + EPS)
-    gain = ag_v[...].astype(F32)[None]
-    normed = [
-        (piece * inverse * gain[:, c * dl : (c + 1) * dl]).astype(BF16)
-        for c, piece in enumerate(pieces)
-    ]
-
-    def project(parts, weight):
-        total = None
-        for c, part in enumerate(parts):
-            term = dot(part, weight[c * dl : (c + 1) * dl, :])
-            total = term if total is None else total + term
-        return total
 
     def project_t(parts, weight):
         total = None
@@ -233,9 +251,9 @@
     def stack(v, count):
         return jnp.concatenate([v[:, k * HD : (k + 1) * HD] for k in range(count)], axis=0)
 
-    key = rope(project_t(normed, wk_v), cosine[:, :kl], signed_sine[:, :kl], front[:, :kl])
-    value = project_t(normed, wv_v)
-    query = rope(project(normed, wq_v), cosine, signed_sine, front)
+    key = rope(key * inverse, cosine[:, :kl], signed_sine[:, :kl], front[:, :kl])
+    value = value * inverse
+    query = rope(query * inverse, cosine, signed_sine, front)
     key = dot(order_k, stack(key, kvl).astype(BF16))
     value = dot(order_k, stack(value, kvl).astype(BF16))
     query = dot(order_q, stack(query, heads).astype(BF16))

time: 34.9 us -> 34.4 us (0.986)
  Pallas kernels: 32.7 us -> 32.1 us
    pallas_call x1, Pallas kernels: 32.7 us -> 32.1 us  [body(): pl.pallas_call(functools.partial(kernel, ns, nt), out_shape=jax.ShapeDtyp...]
where the time goes in v5:
time: 34.4 us; the launch traced here: 34.2 us
  Pallas kernels  32.1 us (93%)
  local copies, waits for them, and re-layouts  1.41 us (4%)
  between operations  0.66 us (2%)
    pallas_call x1, Pallas kernels, body(): pl.pallas_call(functools.partial(kernel, ns, nt), out_shape=jax.ShapeDtyp...  32.1 us
    unnamed x1, local copies, waits for them, and re-layouts  1.41 us

profile of v5, /device:TPU:0, one launch (start us, length us, event | category | flops | bytes accessed | tf_op | source)
XLA Modules:
  0.0 34.2 jit_solution(13220858911937204679)
XLA Ops:
  0.7 32.1 %shard_map.163 = bf16[8,4,640]{2,1,0:T(4,128)(2,1)} custom-call(bf16[8,4,640]{2,1,0:T(4,128)(2,1)} %tok.1, bf16[2560]{0:T(1024)(128)(2,1)} %ag.1, bf16[2560]{0:T(1024)(128)(2,1)} %mg.1, bf16[2560,640]{1,0:T(8,128)(2,1)} %wq.1, bf16[160,2560]{1,0:T(8,128)(2,1)} %bitcast.8, bf16[160,2560]{1,0:T(8,128)(2,1)} %bitcast.9, bf16[640,2560]{1,0:T(8,128)(2,1)} %wo.1, ...), custom_call_target="tpu_custom_call" | custom-call | tf_op jit(solution)/shard_map/pallas_call | solution.py:437
  32.8 1.4 %copy.20 = bf16[8,4,640]{2,1,0:T(4,128)(2,1)} copy(bf16[8,4,640]{2,1,0:T(4,128)(2,1)} %shard_map.163) | data formatting | bytes 81920

commit v6 on v5

--- a/solution.py
+++ b/solution.py
@@ -212,6 +212,32 @@
             copy.wait()
     for copy in later:
         copy.start()
+    short_k = sk_v[...].reshape(short_slots * kvl, sk.shape[2])
+    short_v = sv_v[...].reshape(short_slots * kvl, sv.shape[2])
+    row_count = heads * steps
+    new_count = kvl * steps
+    i = iota((row_count, 1), 0)
+    step_of = i // heads
+    kv_of = i % heads // GROUP
+    new_col = iota((1, new_count), 1)
+    new_mask = (kv_of == new_col // steps) & (new_col % steps <= step_of) & (me_s == 0)
+    lane = iota((row_count, 128), 1)
+
+    def by_kv(terms):
+        total = terms[0]
+        for k in range(1, kvl):
+            total = jnp.where(kv_of == k, terms[k], total)
+        return total
+
+    short_keys = [short_k[:, r * HD : (r + 1) * HD] for r in range(reqs - 1)]
+    short_values = [short_v[:, r * HD : (r + 1) * HD] for r in range(reqs - 1)]
+    slot = me_s * long_slots + iota((1, long_slots), 1)
+    old_masks = [((slot - seen[0]) & (WIN - 1)) > step_of]
+    col = iota((1, short_slots * kvl), 1)
+    slot = me_s * short_slots + col // kvl
+    same_kv = kv_of == col % kvl
+    old_masks += [same_kv & (slot < slen[r]) for r in range(reqs - 1)]
+
     gain = ag_v[...].astype(F32)[None]
     gains = [gain[:, c * dl : (c + 1) * dl] for c in range(nt)]
     square = jnp.zeros((rows, 1), F32)
@@ -258,38 +284,16 @@
     value = dot(order_k, stack(value, kvl).astype(BF16))
     query = dot(order_q, stack(query, heads).astype(BF16))
 
-    short_k = sk_v[...].reshape(short_slots * kvl, sk.shape[2])
-    short_v = sv_v[...].reshape(short_slots * kvl, sv.shape[2])
-    row_count = heads * steps
-    new_count = kvl * steps
-    i = iota((row_count, 1), 0)
-    step_of = i // heads
-    kv_of = i % heads // GROUP
-    new_col = iota((1, new_count), 1)
-    new_mask = (kv_of == new_col // steps) & (new_col % steps <= step_of) & (me_s == 0)
-    lane = iota((row_count, 128), 1)
-
-    def by_kv(terms):
-        total = terms[0]
-        for k in range(1, kvl):
-            total = jnp.where(kv_of == k, terms[k], total)
-        return total
-
     blocks = []
     for r in range(reqs):
         q_r = query[r * row_count : (r + 1) * row_count].astype(BF16)
         k_r = key[r * new_count : (r + 1) * new_count].astype(BF16)
         v_r = value[r * new_count : (r + 1) * new_count].astype(BF16)
+        old_mask = old_masks[r]
         if r == 0:
-            slot = me_s * long_slots + iota((1, long_slots), 1)
-            old_mask = ((slot - seen[0]) & (WIN - 1)) > step_of
             old_dots = by_kv([dot(q_r, lk_v[k]) for k in range(kvl)])
         else:
-            cut = slice((r - 1) * HD, r * HD)
-            col = iota((1, short_slots * kvl), 1)
-            slot = me_s * short_slots + col // kvl
-            old_mask = (kv_of == col % kvl) & (slot < slen[r - 1])
-            old_dots = dot_t(q_r, short_k[:, cut])
+            old_dots = dot_t(q_r, short_keys[r - 1])
         old_score = jnp.where(old_mask, old_dots * SCALE, HIDDEN_SCORE)
         new_score = jnp.where(new_mask, dot_t(q_r, k_r) * SCALE, HIDDEN_SCORE)
         top = jnp.maximum(
@@ -302,7 +306,7 @@
         if r == 0:
             acc = by_kv([dot_t(old_w, lv_v[k]) for k in range(kvl)])
         else:
-            acc = dot(old_w, short_v[:, cut])
+            acc = dot(old_w, short_values[r - 1])
         acc = acc + dot(new_w.astype(BF16), v_r)
         full = jnp.concatenate([acc, jnp.zeros((row_count, 128 - HD), F32)], axis=1)
         terms = []
@@ -343,12 +347,19 @@
     attended = dot(join_heads, attended).astype(BF16)
 
     later[1].wait()
-    head_term = dot(attended, wo_v[...])[:reqs]
-    head_parts = [head_term[:, c * dl : (c + 1) * dl] for c in range(nt)]
-    ob[...] = jnp.concatenate(head_parts, axis=0).astype(BF16)
-    o_copies = [to_pair(ob, orb.at[e - 1], o_send, o_recv, e) for e in range(1, 2 * nt)]
-    for copy in o_copies:
-        copy.start()
+    head_parts, o_copies = [], []
+    per = nt // 2
+    for side in range(2):
+        head_term = dot(attended, wo_v[:, side * per * dl : (side + 1) * per * dl])[:reqs]
+        some = [head_term[:, c * dl : (c + 1) * dl] for c in range(per)]
+        ob[side] = jnp.concatenate(some, axis=0).astype(BF16)
+        head_parts += some
+        for e in range(1, 2 * nt):
+            copy = to_pair(
+                ob.at[side], orb.at[side, e - 1], o_send.at[side], o_recv.at[side], e
+            )
+            copy.start()
+            o_copies.append(copy)
     stream = [a + b for a, b in zip(stream, head_parts)]
     later[0].wait()
     gain = mg_v[...].astype(F32)[None]
@@ -356,10 +367,13 @@
         copy.wait()
 
     def summed(slots):
-        got = orb[slots[0]].astype(F32)
-        for slot in slots[1:]:
-            got = got + orb[slot].astype(F32)
-        return [got[c * reqs : (c + 1) * reqs] for c in range(nt)]
+        parts = []
+        for side in range(2):
+            got = orb[side, slots[0]].astype(F32)
+            for slot in slots[1:]:
+                got = got + orb[side, slot].astype(F32)
+            parts += [got[c * reqs : (c + 1) * reqs] for c in range(per)]
+        return parts
 
     stream = [a + b for a, b in zip(stream, summed(range(nt - 1)))]
     mate_stream = [a + b for a, b in zip(mate_stream, summed(range(nt - 1, 2 * nt - 1)))]
@@ -448,15 +462,15 @@
             pltpu.VMEM((nt, steps, reqs, dl), BF16),
             pltpu.VMEM((steps, m_rows, 128), BF16),
             pltpu.VMEM((ns - 1, m_rows, 128), BF16),
-            pltpu.VMEM((nt * reqs, dl), BF16),
-            pltpu.VMEM((2 * nt - 1, nt * reqs, dl), BF16),
+            pltpu.VMEM((2, nt // 2 * reqs, dl), BF16),
+            pltpu.VMEM((2, 2 * nt - 1, nt // 2 * reqs, dl), BF16),
             pltpu.VMEM((2, nt, reqs, dl), BF16),
             pltpu.VMEM((2 * nt - 1, reqs, dl), BF16),
             pltpu.VMEM((reqs, dl), BF16),
             dma((15 + nt,)),
             dma((nt - 1,)), dma((nt - 1,)),
             dma((ns - 1,)), dma((ns - 1,)),
-            dma((2 * nt - 1,)), dma((2 * nt - 1,)),
+            dma((2, 2 * nt - 1)), dma((2, 2 * nt - 1)),
             dma((2 * nt - 1,)), dma((2 * nt - 1,)),
             dma((steps - 1,)), dma((steps - 1,)),
         ],

time: 34.4 us -> 34.4 us (level)
  no operation moved by 1% of the time
where the time goes in v6:
time: 34.4 us; the launch traced here: 34.2 us
  Pallas kernels  32.2 us (94%)
  local copies, waits for them, and re-layouts  1.41 us (4%)
  between operations  0.66 us (2%)
    pallas_call x1, Pallas kernels, body(): pl.pallas_call(functools.partial(kernel, ns, nt), out_shape=jax.ShapeDtyp...  32.2 us
    unnamed x1, local copies, waits for them, and re-layouts  1.41 us

profile of v6, /device:TPU:0, one launch (start us, length us, event | category | flops | bytes accessed | tf_op | source)
XLA Modules:
  0.0 34.2 jit_solution(7519308995923218446)
XLA Ops:
  0.7 32.2 %shard_map.163 = bf16[8,4,640]{2,1,0:T(4,128)(2,1)} custom-call(bf16[8,4,640]{2,1,0:T(4,128)(2,1)} %tok.1, bf16[2560]{0:T(1024)(128)(2,1)} %ag.1, bf16[2560]{0:T(1024)(128)(2,1)} %mg.1, bf16[2560,640]{1,0:T(8,128)(2,1)} %wq.1, bf16[160,2560]{1,0:T(8,128)(2,1)} %bitcast.8, bf16[160,2560]{1,0:T(8,128)(2,1)} %bitcast.9, bf16[640,2560]{1,0:T(8,128)(2,1)} %wo.1, ...), custom_call_target="tpu_custom_call" | custom-call | tf_op jit(solution)/shard_map/pallas_call | solution.py:451
  32.8 1.4 %copy.20 = bf16[8,4,640]{2,1,0:T(4,128)(2,1)} copy(bf16[8,4,640]{2,1,0:T(4,128)(2,1)} %shard_map.163) | data formatting | bytes 81920

commit v7 on v6

--- a/solution.py
+++ b/solution.py
@@ -267,10 +267,10 @@
         query = query + dot(piece, wq_v[here, :])
     inverse = lax.rsqrt(square * np.float32(1.0 / model) + EPS)
 
-    def project_t(parts, weight):
+    def units_by_rows(parts, weight):
         total = None
         for c, part in enumerate(parts):
-            term = dot_t(part, weight[:, c * dl : (c + 1) * dl])
+            term = dot_t(weight[:, c * dl : (c + 1) * dl], part)
             total = term if total is None else total + term
         return total
 
@@ -387,15 +387,17 @@
         for c, piece in enumerate(both)
     ]
     later[2].wait()
-    gate = project_t(mlp_in, wg_v)
+    gate = units_by_rows(mlp_in, wg_v)
     later[3].wait()
-    lift = project_t(mlp_in, wu_v)
+    lift = units_by_rows(mlp_in, wu_v)
     hidden = gate / (1.0 + jnp.exp(-gate)) * lift
     if 2 * share > ff:
-        shared = (iota((1, share), 1) < 2 * share - ff) & (half == 1)
+        shared = (iota((share, 1), 0) < 2 * share - ff) & (half == 1)
         hidden = jnp.where(shared, 0.0, hidden)
+    identity = one_hot(iota((8, 8), 0) == iota((8, 8), 1))
+    hidden = dot_t(identity, hidden.astype(BF16)).astype(BF16)
     later[4].wait()
-    down = dot(hidden.astype(BF16), wd_v[...])
+    down = dot(hidden, wd_v[...])
     result = jnp.zeros((reqs, dl), F32)
     for c in range(nt):
         piece = down[:, c * dl : (c + 1) * dl]

time: 34.4 us -> 35.9 us (1.044)
  Pallas kernels: 32.2 us -> 33.7 us
    pallas_call x1, Pallas kernels: 32.2 us -> 33.7 us  [body(): pl.pallas_call(functools.partial(kernel, ns, nt), out_shape=jax.ShapeDtyp...]
where the time goes in v7:
time: 35.9 us; the launch traced here: 35.8 us
  Pallas kernels  33.7 us (94%)
  local copies, waits for them, and re-layouts  1.41 us (4%)
  between operations  0.66 us (2%)
    pallas_call x1, Pallas kernels, body(): pl.pallas_call(functools.partial(kernel, ns, nt), out_shape=jax.ShapeDtyp...  33.7 us
    unnamed x1, local copies, waits for them, and re-layouts  1.41 us

profile of v7, /device:TPU:0, one launch (start us, length us, event | category | flops | bytes accessed | tf_op | source)
XLA Modules:
  0.0 35.8 jit_solution(9856538273189615487)
XLA Ops:
  0.7 33.7 %shard_map.163 = bf16[8,4,640]{2,1,0:T(4,128)(2,1)} custom-call(bf16[8,4,640]{2,1,0:T(4,128)(2,1)} %tok.1, bf16[2560]{0:T(1024)(128)(2,1)} %ag.1, bf16[2560]{0:T(1024)(128)(2,1)} %mg.1, bf16[2560,640]{1,0:T(8,128)(2,1)} %wq.1, bf16[160,2560]{1,0:T(8,128)(2,1)} %bitcast.8, bf16[160,2560]{1,0:T(8,128)(2,1)} %bitcast.9, bf16[640,2560]{1,0:T(8,128)(2,1)} %wo.1, ...), custom_call_target="tpu_custom_call" | custom-call | tf_op jit(solution)/shard_map/pallas_call | solution.py:453
  34.3 1.4 %copy.20 = bf16[8,4,640]{2,1,0:T(4,128)(2,1)} copy(bf16[8,4,640]{2,1,0:T(4,128)(2,1)} %shard_map.163) | data formatting | bytes 81920

commit v8 on v5

--- a/solution.py
+++ b/solution.py
@@ -51,6 +51,11 @@
             index = index + bit - 2 * bit * (index // bit % 2)
         bit *= 2
     return index
+
+
+def far_first(copies):
+    order = sorted(range(len(copies)), key=lambda n: abs(2 * n + 1 - len(copies)))
+    return [copies[n] for n in order]
 
 
 def one_hot(condition):
@@ -326,7 +331,7 @@
         s_copies.append(
             to_seq(sb.at[target // copies_of_step], rb.at[d - 1], s_send, s_recv, d, target)
         )
-    for copy in s_copies:
+    for copy in far_first(s_copies):
         copy.start()
     stream = [xg[c, my_step].astype(F32) for c in range(nt)]
     mate_stream = [xg[c, mate_step].astype(F32) for c in range(nt)]
@@ -406,7 +411,7 @@
     for d in range(1, steps):
         target = lax.rem(my_step + d, steps) * copies_of_step + my_twin
         f_copies.append(to_seq(fb, out.at[my_step], f_send, f_recv, d, target))
-    for copy in f_copies:
+    for copy in far_first(f_copies):
         copy.start()
     own = pltpu.make_async_copy(fb, out.at[my_step], local_sem.at[14 + nt])
     own.start()

time: 34.4 us -> 34.6 us (level)
  no operation moved by 1% of the time
where the time goes in v8:
time: 34.6 us; the launch traced here: 34.5 us
  Pallas kernels  32.4 us (94%)
  local copies, waits for them, and re-layouts  1.41 us (4%)
  between operations  0.66 us (2%)
    pallas_call x1, Pallas kernels, body(): pl.pallas_call(functools.partial(kernel, ns, nt), out_shape=jax.ShapeDtyp...  32.4 us
    unnamed x1, local copies, waits for them, and re-layouts  1.41 us

profile of v8, /device:TPU:0, one launch (start us, length us, event | category | flops | bytes accessed | tf_op | source)
XLA Modules:
  0.0 34.5 jit_solution(6928926011307031232)
XLA Ops:
  0.7 32.4 %shard_map.163 = bf16[8,4,640]{2,1,0:T(4,128)(2,1)} custom-call(bf16[8,4,640]{2,1,0:T(4,128)(2,1)} %tok.1, bf16[2560]{0:T(1024)(128)(2,1)} %ag.1, bf16[2560]{0:T(1024)(128)(2,1)} %mg.1, bf16[2560,640]{1,0:T(8,128)(2,1)} %wq.1, bf16[160,2560]{1,0:T(8,128)(2,1)} %bitcast.8, bf16[160,2560]{1,0:T(8,128)(2,1)} %bitcast.9, bf16[640,2560]{1,0:T(8,128)(2,1)} %wo.1, ...), custom_call_target="tpu_custom_call" | custom-call | tf_op jit(solution)/shard_map/pallas_call | solution.py:442
  33.0 1.4 %copy.20 = bf16[8,4,640]{2,1,0:T(4,128)(2,1)} copy(bf16[8,4,640]{2,1,0:T(4,128)(2,1)} %shard_map.163) | data formatting | bytes 81920
